TPU v7x, 256 devices: a whole 4x4x8 slice. The times are simulated.
256 devices in a mesh: docs: 32 (over z, y), cent: 8 (over x, core).
Axes of the slice: x: 4, y: 4, z: 8, core: 2. Of those that a mesh axis runs over, the one named last changes fastest.
Arguments:
- embeddings: bfloat16 [32768, 768], P('docs'), may hold values from -16 to 16
- centroids: bfloat16 [32768, 768], P('cent')
Outputs:
- new_centroids: bfloat16 [8, 4096, 768], P('cent', 'docs')
All inputs are finite; a program needn't handle non-finite values.
Results may differ from a plain program's by a relative error of at most 0.0049.
Values may be sent and summed in bfloat16 or wider, within the bound.
A program may use at most 128 MiB of HBM per device.

v0:
```python
import jax
import jax.numpy as jnp
from jax import lax
from jax.sharding import PartitionSpec as P

PASSES = 3


inv_eps = 10.0
highest = lax.Precision.HIGHEST


def tile_logits(embeddings, centroids):
    return (
        lax.dot_general(
            embeddings, centroids, (((1,), (1,)), ((), ())), preferred_element_type=jnp.float32
        )
        * inv_eps
    )


def row_total(tile, column_scale):
    summed = lax.psum(jnp.dot(tile, column_scale, precision=highest), "cent")
    return summed


def column_total(partial_mass):
    return lax.psum(partial_mass, "docs")


def local(embeddings, centroids):
    docs_count = lax.axis_size("docs")
    total_rows = embeddings.shape[0] * docs_count
    local_cent = centroids.shape[0]
    total_cent = local_cent * lax.axis_size("cent")
    scores = tile_logits(embeddings, centroids)
    top = lax.pmax(jnp.max(scores, axis=1), "cent")
    row = None
    kept = jnp.exp(scores - top[:, None])
    column_scale = jnp.ones((centroids.shape[0],), jnp.float32)
    for step in range(PASSES):
        tile = kept
        row = row_total(tile, column_scale)
        row_weight = 1.0 / (total_rows * row)
        partial_mass = jnp.dot(row_weight, tile, precision=highest)
        if step + 1 < PASSES:
            full_mass = column_total(partial_mass)
            column_scale = 1.0 / (total_cent * full_mass)
            row = None
    weights = (tile * row_weight[:, None]).astype(jnp.bfloat16)
    numerator = lax.dot_general(
        weights, embeddings, (((0,), (0,)), ((), ())), preferred_element_type=jnp.float32
    )
    summed, mass_share = (
        lax.psum_scatter(numerator, "docs", scatter_dimension=0, tiled=True),
        lax.psum_scatter(partial_mass, "docs", scatter_dimension=0, tiled=True),
    )
    result = summed / mass_share[:, None]
    return result.astype(jnp.bfloat16)[None]


def solution(mesh):
    return jax.shard_map(
        local,
        mesh=mesh,
        in_specs=(P("docs", None), P("cent", None)),
        out_specs=P("cent", "docs", None),
        check_vma=False,
    )
```

profile of v0, /device:TPU:64, one launch (start us, length us, event | category | flops | bytes accessed | tf_op | source)
XLA Modules:
  0.0 697.4 jit_solution(450156408587092626)
XLA Ops:
  6.5 0.0 copy-start
  6.5 0.0 reduce-scatter.2.cloned.1.call-start
  6.5 1.4 copy-done
  7.9 13.0 %multiply_reduce_fusion = (f32[1024]{0:T(1024)S(1)}, f32[1024,4096]{1,0:T(8,128)}) fusion(bf16[1024,768]{1,0:T(8,128)(2,1)S(1)} %copy-done, bf16[4096,768]{1,0:T(8,128)(2,1)} %param.3), kind=kOutput, calls=%fused_computation.2 | convolution fusion | flops 6450838528 | bytes 24645632 | tf_op jit(solution)/shard_map/dot_general | solution.py:15
  20.9 14.6 %pmax.7 = f32[1024]{0:T(1024)S(1)} all-reduce(f32[1024]{0:T(1024)S(1)} %get-tuple-element.5), channel_id=1, replica_groups=mesh['docs'=32,'cent'=8] {'cent'}, use_global_device_ids=true, to_apply=%region_1.0 | all-reduce | flops 1024 | bytes 8192 | tf_op jit(solution)/shard_map/pmax | solution.py:37
  35.5 19.8 %fusion.3 = f32[1,1024]{1,0:T(1,128)S(1)} fusion(f32[1024,4096]{1,0:T(8,128)} %get-tuple-element.6, f32[1024]{0:T(1024)S(1)} %pmax.7), kind=kOutput, calls=%fused_computation.9 | convolution fusion | flops 58720256 | bytes 16785408 | tf_op jit(solution)/shard_map/dot_general | solution.py:23
  55.3 12.7 %psum.35 = f32[1024]{0:T(1024)S(1)} all-reduce(f32[1024]{0:T(1024)S(1)} %bitcast.27), channel_id=1, replica_groups=mesh['docs'=32,'cent'=8] {'cent'}, use_global_device_ids=true, to_apply=%region_2.0 | all-reduce | flops 1024 | bytes 8192 | tf_op jit(solution)/shard_map/psum | solution.py:23
  68.0 13.6 %fusion.10 = f32[1,4096]{1,0:T(1,128)S(1)} fusion(f32[1024,1]{0,1:T(1,128)S(1)} %bitcast.31, f32[1024,4096]{1,0:T(8,128)} %get-tuple-element.6, f32[1024]{0:T(1024)S(1)} %pmax.7), kind=kOutput, calls=%fused_computation.19 | convolution fusion | flops 58720256 | bytes 16801792 | tf_op jit(solution)/shard_map/dot_general | solution.py:45
  81.7 133.5 %psum.36 = f32[4096]{0:T(1024)S(1)} all-reduce(f32[4096]{0:T(1024)S(1)} %bitcast.23), channel_id=1, replica_groups=mesh['docs'=32,'cent'=8] {'docs'}, use_global_device_ids=true, to_apply=%region_3.0 | all-reduce | flops 4096 | bytes 32768 | tf_op jit(solution)/shard_map/psum | solution.py:28
  215.2 19.8 %fusion.9 = f32[1,1024]{1,0:T(1,128)S(1)} fusion(f32[4096,1]{0,1:T(1,128)S(1)} %bitcast.25, f32[1024,4096]{1,0:T(8,128)} %get-tuple-element.6, f32[1024]{0:T(1024)S(1)} %pmax.7), kind=kOutput, calls=%fused_computation.18 | convolution fusion | flops 58720256 | bytes 16801792 | tf_op jit(solution)/shard_map/dot_general | solution.py:23
  235.0 12.6 %psum.37 = f32[1024]{0:T(1024)S(1)} all-reduce(f32[1024]{0:T(1024)S(1)} %bitcast.28), channel_id=1, replica_groups=mesh['docs'=32,'cent'=8] {'cent'}, use_global_device_ids=true, to_apply=%region_4.0 | all-reduce | flops 1024 | bytes 8192 | tf_op jit(solution)/shard_map/psum | solution.py:23
  247.6 13.6 %fusion.8 = f32[1,4096]{1,0:T(1,128)S(1)} fusion(f32[1024,1]{0,1:T(1,128)S(1)} %bitcast.32, f32[1024,4096]{1,0:T(8,128)} %get-tuple-element.6, f32[1024]{0:T(1024)S(1)} %pmax.7), kind=kOutput, calls=%fused_computation.17 | convolution fusion | flops 58720256 | bytes 16801792 | tf_op jit(solution)/shard_map/dot_general | solution.py:45
  261.2 137.9 %psum.38 = f32[4096]{0:T(1024)S(1)} all-reduce(f32[4096]{0:T(1024)S(1)} %bitcast.24), channel_id=1, replica_groups=mesh['docs'=32,'cent'=8] {'docs'}, use_global_device_ids=true, to_apply=%region_5.0 | all-reduce | flops 4096 | bytes 32768 | tf_op jit(solution)/shard_map/psum | solution.py:28
  399.1 19.8 %fusion.7 = f32[1,1024]{1,0:T(1,128)S(1)} fusion(f32[4096,1]{0,1:T(1,128)S(1)} %bitcast.26, f32[1024,4096]{1,0:T(8,128)} %get-tuple-element.6, f32[1024]{0:T(1024)S(1)} %pmax.7), kind=kOutput, calls=%fused_computation.16 | convolution fusion | flops 58720256 | bytes 16801792 | tf_op jit(solution)/shard_map/dot_general | solution.py:23
  418.9 12.7 %psum.39 = f32[1024]{0:T(1024)S(1)} all-reduce(f32[1024]{0:T(1024)S(1)} %bitcast.29), channel_id=1, replica_groups=mesh['docs'=32,'cent'=8] {'cent'}, use_global_device_ids=true, to_apply=%region_6.0 | all-reduce | flops 1024 | bytes 8192 | tf_op jit(solution)/shard_map/psum | solution.py:23
  431.6 0.0 copy-start.1
  431.6 14.7 %fusion = f32[4096,768]{1,0:T(8,128)} fusion(bf16[1024,768]{1,0:T(8,128)(2,1)S(1)} %copy-done, f32[1024]{0:T(1024)S(1)} %multiply_divide_fusion.2, f32[1024,4096]{1,0:T(8,128)} %get-tuple-element.6, f32[1024]{0:T(1024)S(1)} %pmax.7), kind=kOutput, calls=%fused_computation.3 | convolution fusion | flops 6459228160 | bytes 30941184 | tf_op jit(solution)/shard_map/dot_general | solution.py:51
  446.3 0.0 reduce-scatter.2.cloned.1.call-update
  446.3 0.0 copy-done.1
  446.3 0.6 dynamic-slice
  447.5 13.6 %fusion.6 = f32[1,4096]{1,0:T(1,128)S(1)} fusion(f32[1024,1]{0,1:T(1,128)S(1)} %bitcast.30, f32[1024,4096]{1,0:T(8,128)} %get-tuple-element.6, f32[1024]{0:T(1024)S(1)} %pmax.7), kind=kOutput, calls=%fused_computation.15 | convolution fusion | flops 58720256 | bytes 16801792 | tf_op jit(solution)/shard_map/dot_general | solution.py:45
  461.2 138.1 %all-reduce = f32[4096]{0:T(1024)S(1)} all-reduce(f32[4096]{0:T(1024)S(1)} %bitcast.22), channel_id=3, replica_groups=mesh['docs'=32,'cent'=8] {'docs'}, use_global_device_ids=true, to_apply=%region_8.0.clone | all-reduce | flops 4096 | bytes 32768
  599.3 0.1 dynamic-slice.1
  599.4 89.1 %reduce-scatter.2.cloned.1.call-done = f32[128,768]{1,0:T(8,128)} async-done(((f32[4096,768]{1,0:T(8,128)}), f32[128,768]{1,0:T(8,128)}) %reduce-scatter.2.cloned.1.call-update) | async-done | bytes 393232 | tf_op jit(solution)/shard_map/reduce_scatter | solution.py:55
  688.5 1.8 fusion.2
  (5 shorter events, 0.0 us)
Async XLA Ops:
  6.5 1.4 copy-start
  6.5 681.9 %reduce-scatter.2.cloned.1.call-start = ((), (), s32[]{:S(2)}) async-start(), calls=%async_computation.1 | async-start | bytes 12976128 | tf_op jit(solution)/shard_map/reduce_scatter | solution.py:55
  431.6 14.7 %copy-start.1 = (u32[256]{0:T(256)S(1)}, u32[256]{0:T(256)}, u32[]{:S(2)}) copy-start(u32[256]{0:T(256)} %constant.12) | copy-start | bytes 3076
Sparse Core Ops, SparseCore 0:
  446.4 242.0 reduce-scatter.1
where the time goes:
time: 706 us; the launch traced here: 697 us
  blocking collectives  462 us (65%)
  matrix products  128 us (18%)
  waiting for transfers between devices  89.1 us (13%)
  between operations  14.4 us (2%)
    psum x2, blocking collectives, column_total(): return lax.psum(partial_mass, 'docs')  271 us
    unnamed x1, blocking collectives  138 us
    reduce_scatter x1, waiting for transfers between devices, local(): lax.psum_scatter(numerator, 'docs', scatter_dimension=0, tiled=True)  89.1 us
    dot_general x3, matrix products, row_total(): summed = lax.psum(jnp.dot(tile, column_scale, precision=highest), 'cent')  59.4 us
    dot_general x3, matrix products, local(): partial_mass = jnp.dot(row_weight, tile, precision=highest)  40.9 us
    psum x3, blocking collectives, row_total(): summed = lax.psum(jnp.dot(tile, column_scale, precision=highest), 'cent')  37.9 us
    dot_general x1, matrix products, local(): lax.dot_general(weights, embeddings, (((0,), (0,)), ((), ())), preferred_...  14.7 us
    pmax x1, blocking collectives, local(): top = lax.pmax(jnp.max(scores, axis=1), 'cent')  14.6 us
  transfers between devices with their start and end apart: 1, of which 1 were waited for; matrix products, arithmetic and copies ran while one was open for 2% of the time, Pallas kernels for 0%

commit v1 on v0

v1 whole, which is shorter than its diff:
```python
import jax
import jax.numpy as jnp
import numpy as np
from jax import lax
from jax.experimental import pallas as pl
from jax.experimental.pallas import tpu as pltpu
from jax.sharding import PartitionSpec as P

MESH = pl.DeviceIdType.MESH
F32 = jnp.float32
BF16 = jnp.bfloat16

NX, NY, NZ = 4, 4, 8
D = 768
PIECE = 64
NB, BW = 8, 512
CH = 128
C = NZ * CH
TOTAL = 32768.0
EXP2_SCALE = 10.0 * float(np.log2(np.e))

ORDER = (4, 3, -3, 2, -2, 1, -1, 0)
POS = {q: i for i, q in enumerate(ORDER)}


def body(
    emb_hbm, cen_hbm, out_ref,
    emb, cen, kern, buf0, buf1,
    st, st2, r0a, r0b, rl, rl2, ra, rb, fac, rw, part, scol, ml, mr, w0, w1, num, snd, rcv,
    ld_sem, ag_s, ag_r, r1_s, r1_r, r2_s, r2_r, m_s, m_r, rs_s, rs_r,
):
    docs = lax.axis_index("docs")
    cent = lax.axis_index("cent")
    z, y = docs // NY, docs % NY
    x, c = cent // 2, cent % 2

    def at(dz=0, dy=0, dx=0, flip=False):
        zz = (z + dz + NZ) % NZ
        yy = (y + dy + NY) % NY
        xx = (x + dx + NX) % NX
        return (zz * NY + yy, xx * 2 + ((1 - c) if flip else c))

    load_e = pltpu.make_async_copy(emb_hbm, emb.at[pl.ds(y * 16, 16)], ld_sem.at[0])
    load_c = pltpu.make_async_copy(cen_hbm.at[:, y], cen, ld_sem.at[1])
    load_e.start()
    load_c.start()

    cent_peers = [(docs, (cent + k) % 8) for k in range(1, 8)]
    y_peers = [at(dy=k) for k in range(1, NY)]
    z_peers = [at(dz=k) for k in range(1, NZ)]
    barrier = pltpu.get_barrier_semaphore()
    for peer in cent_peers + y_peers + z_peers:
        pl.semaphore_signal(barrier, inc=1, device_id=peer, device_id_type=MESH)
    pl.semaphore_wait(barrier, len(cent_peers) + len(y_peers) + len(z_peers))

    def piece(dy, h, dx):
        return ((y + dy + NY) % NY) * 16 + h * 8 + ((x + dx + NX) % NX) * 2 + c

    ag = {}

    def send(name, where, target):
        i = len(ag)
        copy = pltpu.make_async_remote_copy(
            src_ref=emb.at[where], dst_ref=emb.at[where], send_sem=ag_s.at[i], recv_sem=ag_r.at[i],
            device_id=target, device_id_type=MESH,
        )
        copy.start()
        ag[name] = copy

    def got(*names):
        for name in names:
            ag[name].wait_recv()

    def to_sibling(*pieces):
        for dy, h, dx in pieces:
            send(("s", dy, h, dx), piece(dy, h, dx), at(flip=True))

    def to_x(*pieces):
        for dy, h, dx in pieces:
            for s in (1, -1):
                send(("x1", s, dy, h), piece(dy, h, dx), at(dx=s))

    def block_ready(dy, h):
        for dx in range(NX):
            got(("s", dy, h, dx if dx < 3 else -1))

    load_e.wait()
    for s in (1, -1):
        send(("u", s), piece(0, 1, 0), at(dy=s))
    for s in (1, -1):
        send(("l", s), piece(0, 0, 0), at(dy=s))
    for s in (1, -1):
        send(("k", s, 1), piece(0, 0, 1), at(dy=s))
    load_c.wait()

    def phase_1():
        for s in (1, -1):
            got(("u", s))
            to_x((-s, 1, 0))
        for s in (1, -1):
            got(("l", s))
        send(("y3", 1), piece(-1, 0, 0), at(dy=1))
        send(("y3", -1), piece(1, 1, 0), at(dy=-1))
        for k in (2, -1):
            for s in (1, -1):
                send(("k", s, k), piece(0, 0, k), at(dy=s))
        to_sibling((1, 1, 0), (-1, 1, 0), (1, 0, 0), (-1, 0, 0))

    def phase_2():
        got(("y3", 1), ("y3", -1))
        to_x((2, 0, 0), (2, 1, 0))
        to_sibling((2, 0, 0), (2, 1, 0))
        got(("x1", 1, 1, 1), ("x1", -1, -1, 1))
        send(("x2", 1, 1, 1), piece(1, 1, -1), at(dx=1))
        send(("x2", -1, -1, 1), piece(-1, 1, 1), at(dx=-1))
        to_sibling((1, 1, -1), (-1, 1, 1))
        got(("x1", 1, -1, 1), ("x1", -1, 1, 1))
        to_sibling((-1, 1, -1), (1, 1, 1))
        for s in (1, -1):
            got(("k", s, 1))
            to_sibling((-s, 0, 1))

    def phase_3():
        for k in (2, -1):
            for s in (1, -1):
                got(("k", s, k))
                to_sibling((-s, 0, k))

    def phase_4():
        got(("x1", 1, 2, 0), ("x1", -1, 2, 1))
        send(("x2", 1, 2, 0), piece(2, 0, -1), at(dx=1))
        send(("x2", -1, 2, 1), piece(2, 1, 1), at(dx=-1))
        to_sibling((2, 0, -1), (2, 1, 1))
        got(("x1", 1, 2, 1), ("x1", -1, 2, 0))
        to_sibling((2, 1, -1), (2, 0, 1))
        got(("x2", 1, 1, 1), ("x2", -1, -1, 1))
        to_sibling((1, 1, 2), (-1, 1, 2))

    def phase_5():
        got(("x2", 1, 2, 0), ("x2", -1, 2, 1))
        to_sibling((2, 0, 2), (2, 1, 2))

    def block_at(dy, h):
        return ((y + dy + NY) % NY) * 2 + h

    def step(new, new_buf, old, old_buf, old_max):
        if old is not None:
            top = jnp.max(old_max, axis=0, keepdims=True)
            total = jnp.zeros((8, BW), F32)
        new_max = None
        if new is not None:
            e = emb[pl.ds(new * 8, 8)].reshape(BW, D)
        for i in range(4):
            rows = slice(256 * i, 256 * i + 256)
            if new is not None:
                raw = lax.dot_general(
                    cen[2 * i:2 * i + 2].reshape(256, D), e, (((1,), (1,)), ((), ())),
                    preferred_element_type=F32,
                )
                new_buf[rows, :] = raw
                high = jnp.max(raw.reshape(32, 8, BW), axis=0)
                new_max = high if new_max is None else jnp.maximum(new_max, high)
            if old is not None:
                value = jnp.exp2((old_buf[rows, :] - top) * EXP2_SCALE)
                kern[old, rows, :] = value
                total = total + jnp.sum(value.reshape(32, 8, BW), axis=0)
        if old is not None:
            st[0, pl.ds(old, 1), :] = top
            st[1, pl.ds(old, 1), :] = jnp.sum(total, axis=0, keepdims=True)
        return new_max

    blocks = ((0, 0), (0, 1), (1, 0), (-1, 0), (1, 1), (-1, 1), (2, 0), (2, 1))
    before = {1: phase_1, 2: lambda: (phase_2(), phase_3()), 4: phase_4, 6: phase_5}
    bufs = (buf0, buf1)
    high = None
    for i in range(NB + 1):
        if i in before:
            before[i]()
        if 2 <= i < NB:
            block_ready(*blocks[i])
        new = block_at(*blocks[i]) if i < NB else None
        old = block_at(*blocks[i - 1]) if i > 0 else None
        high = step(new, bufs[i % 2], old, bufs[(i + 1) % 2], high)

    def push(src, dst, peers, ssem, rsem):
        copies = []
        for k, peer in enumerate(peers):
            copy = pltpu.make_async_remote_copy(
                src_ref=src, dst_ref=dst.at[k], send_sem=ssem.at[k], recv_sem=rsem.at[k],
                device_id=peer, device_id_type=MESH,
            )
            copy.start()
            copies.append(copy)
        return copies

    sent = []

    def exchange(src, dst, peers, ssem, rsem):
        copies = push(src, dst, peers, ssem, rsem)
        for copy in copies:
            copy.wait_recv()
        sent.extend(copies)

    def merge(own, others, n):
        top = own[0]
        for k in range(n):
            top = jnp.maximum(top, others[k, 0])
        total = own[1] * jnp.exp2((own[0] - top) * EXP2_SCALE)
        for k in range(n):
            total = total + others[k, 1] * jnp.exp2((others[k, 0] - top) * EXP2_SCALE)
        return top, total

    exchange(st, r0a, cent_peers, r1_s.at[0], r1_r.at[0])
    top, total = merge(st, r0a, 7)
    st2[0] = top
    st2[1] = total
    exchange(st2, r0b, y_peers, r2_s.at[0], r2_r.at[0])
    top, total = merge(st2, r0b, 3)
    factor = jnp.exp2((st[0] - top) * EXP2_SCALE)
    fac[...] = factor
    rw[...] = factor / (TOTAL * total)

    def mass_of(n):
        def chunk(g, _):
            rows = pl.ds(pl.multiple_of(g * 64, 64), 64)
            acc = jnp.zeros((64, 128), F32)
            for b in range(NB):
                for l in range(BW // 128):
                    lanes = slice(l * 128, l * 128 + 128)
                    acc = acc + kern[b, rows, lanes] * rw[b:b + 1, lanes]
            part[rows, :] = acc
            return 0

        lax.fori_loop(0, C // 64, chunk, 0)
        for t in range(NZ):
            ml[n, t:t + 1, :] = jnp.sum(part[t * CH:(t + 1) * CH, :].T, axis=0, keepdims=True)

    def summed(own, others, n):
        total = own
        for k in range(n):
            total = total + others[k]
        return total

    for n in range(2):
        mass_of(n)
        exchange(ml.at[n], mr.at[n], z_peers, m_s.at[n], m_r.at[n])
        scale = 1.0 / (TOTAL * summed(ml[n], mr.at[n], 7))
        for t in range(NZ):
            scol[t * CH:(t + 1) * CH, :] = jnp.broadcast_to(scale[t:t + 1, :], (CH, CH)).T

        def row_block(b, _):
            def chunk(g, acc):
                rows = pl.ds(pl.multiple_of(g * 128, 128), 128)
                s = scol[rows, :]
                value = kern[b, rows, :] * jnp.concatenate([s] * (BW // 128), axis=1)
                return acc + jnp.sum(value.reshape(16, 8, BW), axis=0)

            acc = lax.fori_loop(0, C // 128, chunk, jnp.zeros((8, BW), F32))
            rl[n, pl.ds(b, 1), :] = jnp.sum(acc, axis=0, keepdims=True) * fac[pl.ds(b, 1), :]
            return 0

        lax.fori_loop(0, NB, row_block, 0)
        exchange(rl.at[n], ra.at[n], cent_peers, r1_s.at[n + 1], r1_r.at[n + 1])
        rl2[n] = summed(rl[n], ra.at[n], 7)
        exchange(rl2.at[n], rb.at[n], y_peers, r2_s.at[n + 1], r2_r.at[n + 1])
        rw[...] = fac[...] / (TOTAL * summed(rl2[n], rb.at[n], 3))

    ws = (w0, w1)

    def weigh(pair, j):
        q = ORDER[2 * pair + j]
        t = (z + q + NZ) % NZ
        rows = pl.ds(pl.multiple_of(t * CH, CH), CH)
        acc = jnp.zeros((CH, 128), F32)
        for b in range(NB):
            for l in range(BW // 128):
                lanes = slice(l * 128, l * 128 + 128)
                value = kern[b, rows, lanes] * rw[b:b + 1, lanes]
                acc = acc + value
                ws[pair % 2][j * CH:(j + 1) * CH, b * BW + l * 128:b * BW + (l + 1) * 128] = value.astype(BF16)
        ml[2, pl.ds(t, 1), :] = jnp.sum(acc.T, axis=0, keepdims=True)

    def multiply(pair):
        e = emb[...].reshape(NB * BW, D)
        num[2 * pair:2 * pair + 2] = jnp.dot(
            ws[pair % 2][...], e, preferred_element_type=F32
        ).reshape(2, CH, D)

    rs = {}

    def hop(name, q, rows, before=None):
        chain, sign = name[0], (1 if name[0] in ("RA", "RB") else -1)
        i = len(rs)
        value = num[POS[q], rows, :]
        if before is not None:
            rs[before].wait_recv()
            value = value + rcv[slot[before]].astype(F32)
        snd[i] = value.astype(BF16)
        slot[name] = i
        copy = pltpu.make_async_remote_copy(
            src_ref=snd.at[i], dst_ref=rcv.at[i], send_sem=rs_s.at[i], recv_sem=rs_r.at[i],
            device_id=at(dz=sign), device_id_type=MESH,
        )
        copy.start()
        rs[name] = copy

    slot = {}
    lo, hi = slice(0, 64), slice(64, 128)
    weigh(0, 0)
    weigh(0, 1)
    for pair in range(4):
        multiply(pair)
        if pair < 3:
            weigh(pair + 1, 0)
            weigh(pair + 1, 1)
        if pair == 0:
            hop(("RB", 0), 4, lo)
            hop(("LB", 0), 4, hi)
            hop(("RA", 1), 3, hi)
        elif pair == 1:
            hop(("LA", 1), -3, lo)
        elif pair == 2:
            last = push(ml.at[2], mr.at[2], z_peers, m_s.at[2], m_r.at[2])
            sent.extend(last)
            hop(("RB", 1), 3, lo, ("RB", 0))
            hop(("LB", 1), -3, hi, ("LB", 0))
    hop(("RA", 2), 2, hi, ("RA", 1))
    hop(("LA", 2), -2, lo, ("LA", 1))
    hop(("RB", 2), 2, lo, ("RB", 1))
    hop(("LB", 2), -2, hi, ("LB", 1))
    hop(("RA", 3), 1, hi, ("RA", 2))
    hop(("LA", 3), -1, lo, ("LA", 2))
    hop(("RB", 3), 1, lo, ("RB", 2))
    hop(("LB", 3), -1, hi, ("LB", 2))

    for copy in last:
        copy.wait_recv()
    mass = ml[2, pl.ds(z, 1), :]
    for k in range(7):
        mass = mass + mr[2, k, pl.ds(z, 1), :]
    column = jnp.broadcast_to(mass, (CH, CH)).T
    column = jnp.concatenate([column] * (D // CH), axis=1)
    for rows, one, two in ((hi, ("RA", 3), ("LB", 3)), (lo, ("LA", 3), ("RB", 3))):
        rs[one].wait_recv()
        rs[two].wait_recv()
        total = num[POS[0], rows, :] + rcv[slot[one]].astype(F32) + rcv[slot[two]].astype(F32)
        out_ref[rows, :] = (total / column[rows, :]).astype(BF16)

    for copy in list(ag.values()) + sent + list(rs.values()):
        copy.wait_send()


def local(embeddings, centroids):
    e = embeddings.reshape(16, PIECE, D)
    k = centroids.reshape(NZ, NY, CH, D)
    dma = pltpu.SemaphoreType.DMA
    v = pltpu.VMEM
    out = pl.pallas_call(
        body,
        out_shape=jax.ShapeDtypeStruct((CH, D), BF16),
        in_specs=[pl.BlockSpec(memory_space=pl.ANY)] * 2,
        out_specs=pl.BlockSpec(memory_space=pltpu.VMEM),
        scratch_shapes=[
            v((64, PIECE, D), BF16), v((NZ, CH, D), BF16), v((NB, C, BW), F32), v((C, BW), F32), v((C, BW), F32),
            v((2, NB, BW), F32), v((2, NB, BW), F32), v((7, 2, NB, BW), F32), v((3, 2, NB, BW), F32),
            v((2, NB, BW), F32), v((2, NB, BW), F32), v((2, 7, NB, BW), F32), v((2, 3, NB, BW), F32),
            v((NB, BW), F32), v((NB, BW), F32), v((C, 128), F32), v((C, 128), F32),
            v((3, NZ, CH), F32), v((3, 7, NZ, CH), F32),
            v((2 * CH, NB * BW), BF16), v((2 * CH, NB * BW), BF16), v((NZ, CH, D), F32),
            v((14, 64, D), BF16), v((14, 64, D), BF16),
            dma((2,)), dma((48,)), dma((48,)), dma((3, 7)), dma((3, 7)), dma((3, 3)), dma((3, 3)),
            dma((3, 7)), dma((3, 7)), dma((14,)), dma((14,)),
        ],
        compiler_params=pltpu.CompilerParams(
            collective_id=0, has_side_effects=True, vmem_limit_bytes=60 * 1024 * 1024
        ),
        cost_estimate=pl.CostEstimate(
            flops=4 * C * NB * BW * D, bytes_accessed=8 * 1024 * 1024, transcendentals=C * NB * BW
        ),
    )(e, k)
    return out[None]


def solution(mesh):
    return jax.shard_map(
        local,
        mesh=mesh,
        in_specs=(P("docs", None), P("cent", None)),
        out_specs=P("cent", "docs", None),
        check_vma=False,
    )
```

time: 706 us -> 102 us (0.14); the launches traced: 697 us -> 101 us
  blocking collectives: 462 us -> 0 us
  matrix products: 128 us -> 0 us
  Pallas kernels: 0 us -> 99.2 us
  waiting for transfers between devices: 89.1 us -> 0 us
  between operations: 14.4 us -> 0.01 us
    psum x5 -> x0, blocking collectives: 309 us -> none  [the longest x2 271 us: column_total(): return lax.psum(partial_mass, 'docs')]
    unnamed x1 -> x0, blocking collectives: 138 us -> none
    dot_general x8 -> x0, matrix products: 128 us -> none  [the longest x3 59.4 us: row_total(): summed = lax.psum(jnp.dot(tile, column_scale, precision=highest), 'cent')]
    pallas_call x0 -> x1, Pallas kernels: none -> 99.2 us  [local(): pl.pallas_call(body, out_shape=jax.ShapeDtypeStruct((CH, D), BF16), in_sp...]
    reduce_scatter x1 -> x0, waiting for transfers between devices: 89.1 us -> none  [local(): lax.psum_scatter(numerator, 'docs', scatter_dimension=0, tiled=True)]
    pmax x1 -> x0, blocking collectives: 14.6 us -> none  [local(): top = lax.pmax(jnp.max(scores, axis=1), 'cent')]
  transfers between devices with their start and end apart: 1 -> 0, of which waited for: 1 -> 0; matrix products, arithmetic and copies ran while one was open for 2% -> 0% of each run, Pallas kernels for 0% -> 0%
where the time goes in v1:
time: 102 us; the launch traced here: 101 us
  Pallas kernels  99.2 us (97%)
  local copies, waits for them, and re-layouts  1.62 us (2%)
    pallas_call x1, Pallas kernels, local(): pl.pallas_call(body, out_shape=jax.ShapeDtypeStruct((CH, D), BF16), in_sp...  99.2 us

profile of v1, /device:TPU:64, one launch (start us, length us, event | category | flops | bytes accessed | tf_op | source)
XLA Modules:
  0.0 100.9 jit_solution(2082082637358446864)
XLA Ops:
  0.0 99.2 %shard_map.28 = bf16[128,768]{1,0:T(8,128)(2,1)} custom-call(bf16[16,64,768]{2,1,0:T(8,128)(2,1)} %bitcast.5, bf16[8,4,128,768]{3,2,1,0:T(8,128)(2,1)} %bitcast.4), custom_call_target="tpu_custom_call" | custom-call | flops 12884901888 | bytes 8388608 | tf_op jit(solution)/shard_map/pallas_call | solution.py:358
  99.2 1.6 %copy.4 = bf16[1,128,768]{2,1,0:T(8,128)(2,1)} copy(bf16[1,128,768]{2,1,0:T(8,128)(2,1)} %bitcast.3) | data formatting | bytes 393216

commit v2 on v1

v2 whole, which is shorter than its diff:
```python
import jax
import jax.numpy as jnp
import numpy as np
from jax import lax
from jax.experimental import pallas as pl
from jax.experimental.pallas import tpu as pltpu
from jax.sharding import PartitionSpec as P

MESH = pl.DeviceIdType.MESH
F32 = jnp.float32
BF16 = jnp.bfloat16

NX, NY, NZ = 4, 4, 8
D = 768
PIECE = 64
NB, BW = 8, 512
CH = 128
C = NZ * CH
TOTAL = 32768.0
EXP2_SCALE = 10.0 * float(np.log2(np.e))

GROUPS = ((4,), (3, -3), (2, -2), (1, -1), (0,))
POS = {q: i for i, q in enumerate(q for group in GROUPS for q in group)}
LN2 = float(np.log(2.0))


def body(
    emb_hbm, cen_hbm, out_ref,
    emb, cen, kern, buf0, buf1,
    top_of, rl, rl2, ra, rb, fac, rw, part, scol, ml, mr, w0, w1, num, snd, rcv,
    ld_sem, ag_s, ag_r, r1_s, r1_r, r2_s, r2_r, m_s, m_r, rs_s, rs_r,
):
    docs = lax.axis_index("docs")
    cent = lax.axis_index("cent")
    z, y = docs // NY, docs % NY
    x, c = cent // 2, cent % 2

    def at(dz=0, dy=0, dx=0, flip=False):
        zz = (z + dz + NZ) % NZ
        yy = (y + dy + NY) % NY
        xx = (x + dx + NX) % NX
        return (zz * NY + yy, xx * 2 + ((1 - c) if flip else c))

    load_e = pltpu.make_async_copy(emb_hbm, emb.at[pl.ds(y * 16, 16)], ld_sem.at[0])
    load_c = pltpu.make_async_copy(cen_hbm.at[:, y], cen, ld_sem.at[1])
    load_e.start()
    load_c.start()

    cent_peers = [(docs, (cent + k) % 8) for k in range(1, 8)]
    y_peers = [at(dy=k) for k in range(1, NY)]
    z_peers = [at(dz=k) for k in range(1, NZ)]
    barrier = pltpu.get_barrier_semaphore()
    for peer in cent_peers + y_peers + z_peers:
        pl.semaphore_signal(barrier, inc=1, device_id=peer, device_id_type=MESH)
    pl.semaphore_wait(barrier, len(cent_peers) + len(y_peers) + len(z_peers))

    def piece(dy, h, dx):
        return ((y + dy + NY) % NY) * 16 + h * 8 + ((x + dx + NX) % NX) * 2 + c

    ag = {}

    def send(name, where, target, src=None):
        i = len(ag)
        copy = pltpu.make_async_remote_copy(
            src_ref=emb.at[where] if src is None else src, dst_ref=emb.at[where],
            send_sem=ag_s.at[i], recv_sem=ag_r.at[i], device_id=target, device_id_type=MESH,
        )
        copy.start()
        ag[name] = copy

    def send_own(name, h, dx, s):
        send(name, piece(0, h, dx), at(dy=s), emb_hbm.at[h * 8 + ((x + dx + NX) % NX) * 2 + c])

    def got(*names):
        for name in names:
            ag[name].wait_recv()

    def to_sibling(*pieces):
        for dy, h, dx in pieces:
            send(("s", dy, h, dx), piece(dy, h, dx), at(flip=True))

    def to_x(*pieces):
        for s, dy, h in pieces:
            send(("x1", s, dy, h), piece(dy, h, 0), at(dx=s))

    def block_ready(dy, h):
        for dx in (0, 1, 2, -1):
            got(("s", dy, h, dx))

    send_own(("f", 1), 1, 0, 1)
    send_own(("f", -1), 0, 0, -1)
    send_own(("g", 1), 0, 0, 1)
    send_own(("g", -1), 1, 0, -1)
    load_e.wait()
    load_c.wait()

    def phase_a():
        got(("f", 1), ("f", -1))
        to_x((1, -1, 1), (-1, -1, 1))
        send(("y3", 1), piece(-1, 1, 0), at(dy=1))
        send(("y3", -1), piece(1, 0, 0), at(dy=-1))
        for k in (1, 2, -1):
            for s in (1, -1):
                send_own(("k", s, k), 0, k, s)
        to_sibling((-1, 1, 0), (1, 0, 0))

    def phase_b():
        got(("g", 1), ("g", -1))
        to_x((1, 1, 1), (-1, 1, 1))
        to_sibling((-1, 0, 0), (1, 1, 0))

    def phase_c():
        got(("x1", -1, -1, 1), ("x1", 1, -1, 1))
        send(("x2", -1, -1, 1), piece(-1, 1, 1), at(dx=-1))
        to_sibling((-1, 1, 1), (-1, 1, -1))
        got(("x1", 1, 1, 1), ("x1", -1, 1, 1))
        send(("x2", 1, 1, 1), piece(1, 1, -1), at(dx=1))
        to_sibling((1, 1, -1), (1, 1, 1))
        got(("y3", 1), ("y3", -1))
        to_x((1, 2, 0), (-1, 2, 1), (1, 2, 1), (-1, 2, 0))
        to_sibling((2, 1, 0), (2, 0, 0))
        got(("x2", 1, 1, 1), ("x2", -1, -1, 1))
        to_sibling((1, 1, 2), (-1, 1, 2))

    def phase_f():
        for k in (1, 2):
            got(("k", 1, k), ("k", -1, k))
            to_sibling((1, 0, k), (-1, 0, k))

    def phase_g():
        got(("x1", 1, 2, 0), ("x1", -1, 2, 1))
        send(("x2", 1, 2, 0), piece(2, 0, -1), at(dx=1))
        send(("x2", -1, 2, 1), piece(2, 1, 1), at(dx=-1))
        to_sibling((2, 0, -1), (2, 1, 1))
        got(("k", 1, -1), ("k", -1, -1))
        to_sibling((1, 0, -1), (-1, 0, -1))

    def phase_h():
        got(("x1", 1, 2, 1), ("x1", -1, 2, 0))
        to_sibling((2, 1, -1), (2, 0, 1))

    def phase_i():
        got(("x2", 1, 2, 0), ("x2", -1, 2, 1))
        to_sibling((2, 0, 2), (2, 1, 2))

    sent = []

    def push(src, dst, peers, ssem, rsem):
        copies = []
        for k, peer in enumerate(peers):
            copy = pltpu.make_async_remote_copy(
                src_ref=src, dst_ref=dst.at[k], send_sem=ssem.at[k], recv_sem=rsem.at[k],
                device_id=peer, device_id_type=MESH,
            )
            copy.start()
            copies.append(copy)
        sent.extend(copies)
        return copies

    def landed(copies):
        for copy in copies:
            copy.wait_recv()

    def push_1(n, half):
        return push(rl.at[n, half], ra.at[n, half], cent_peers, r1_s.at[n, half], r1_r.at[n, half])

    def push_2(n, half):
        return push(rl2.at[n, half], rb.at[n, half], y_peers, r2_s.at[n, half], r2_r.at[n, half])

    def summed(own, others, n):
        total = own
        for k in range(n):
            total = total + others[k]
        return total

    def log_summed(own, others, n):
        top = own
        for k in range(n):
            top = jnp.maximum(top, others[k])
        total = jnp.exp2(own - top)
        for k in range(n):
            total = total + jnp.exp2(others[k] - top)
        return top + jnp.log(total) * (1.0 / LN2)

    def block_at(dy, h):
        return ((y + dy + NY) % NY) * 2 + h

    blocks = ((0, 0), (0, 1), (1, 1), (-1, 1), (1, 0), (-1, 0), (2, 0), (2, 1))
    bufs = (buf0, buf1)
    highs = {}

    def step(new, old):
        if old is not None:
            top = jnp.max(highs[old], axis=0, keepdims=True)
            total = jnp.zeros((8, BW), F32)
            old_buf, place = bufs[old % 2], block_at(*blocks[old])
        if new is not None:
            e = emb[pl.ds(block_at(*blocks[new]) * 8, 8)].reshape(BW, D)
            new_buf, new_max = bufs[new % 2], None
        for i in range(4):
            rows = slice(256 * i, 256 * i + 256)
            if new is not None:
                raw = lax.dot_general(
                    cen[2 * i:2 * i + 2].reshape(256, D), e, (((1,), (1,)), ((), ())),
                    preferred_element_type=F32,
                )
                new_buf[rows, :] = raw
                high = jnp.max(raw.reshape(32, 8, BW), axis=0)
                new_max = high if new_max is None else jnp.maximum(new_max, high)
            if old is not None:
                value = jnp.exp2((old_buf[rows, :] - top) * EXP2_SCALE)
                kern[place, rows, :] = value
                total = total + jnp.sum(value.reshape(32, 8, BW), axis=0)
        if new is not None:
            highs[new] = new_max
        if old is not None:
            scaled = top * EXP2_SCALE
            whole = scaled + jnp.log(jnp.sum(total, axis=0, keepdims=True)) * (1.0 / LN2)
            for j in range(2):
                lanes = slice(256 * j, 256 * j + 256)
                r = (old % 4) * 2 + j
                rl[0, old // 4, r:r + 1, :] = whole[:, lanes]
                top_of[place // 4, pl.ds((place % 4) * 2 + j, 1), :] = scaled[:, lanes]

    step(0, None)
    phase_a()
    step(1, 0)
    phase_b()
    step(None, 1)
    phase_c()
    block_ready(*blocks[2])
    step(2, None)
    phase_f()
    block_ready(*blocks[3])
    step(3, 2)
    phase_g()
    block_ready(*blocks[4])
    step(4, 3)
    first = push_1(0, 0)
    phase_h()
    block_ready(*blocks[5])
    step(5, 4)
    phase_i()
    block_ready(*blocks[6])
    step(6, 5)
    block_ready(*blocks[7])
    step(7, 6)
    step(None, 7)
    second = push_1(0, 1)
    for half, copies in ((0, first), (1, second)):
        landed(copies)
        merged = log_summed(rl[0, half], ra.at[0, half], 7)
        for j in range(8):
            place = block_at(*blocks[4 * half + j // 2])
            rl2[0, place // 4, pl.ds((place % 4) * 2 + j % 2, 1), :] = merged[j:j + 1, :]
    first, second = push_2(0, 0), push_2(0, 1)

    def start_weights(half):
        whole = log_summed(rl2[0, half], rb.at[0, half], 3)
        factor = jnp.exp2(top_of[half] - whole)
        fac[half] = factor
        rw[half] = factor * (1.0 / TOTAL)

    landed(first)
    start_weights(0)

    def weighted(b, rows, l):
        r = (b % 4) * 2 + l // 2
        w = rw[b // 4, r:r + 1, (l % 2) * 128:(l % 2) * 128 + 128]
        return kern[b, rows, l * 128:l * 128 + 128] * w

    def mass_half(half):
        def chunk(g, _):
            rows = pl.ds(pl.multiple_of(g * 64, 64), 64)
            acc = jnp.zeros((64, 128), F32) if half == 0 else part[rows, :]
            for b in range(4 * half, 4 * half + 4):
                for l in range(BW // 128):
                    acc = acc + weighted(b, rows, l)
            part[rows, :] = acc
            return 0

        lax.fori_loop(0, C // 64, chunk, 0)

    def row_half(n, half):
        def row_block(b, _):
            def chunk(g, acc):
                rows = pl.ds(pl.multiple_of(g * 128, 128), 128)
                s = scol[rows, :]
                value = kern[4 * half + b, rows, :] * jnp.concatenate([s] * (BW // 128), axis=1)
                return acc + jnp.sum(value.reshape(16, 8, BW), axis=0)

            acc = lax.fori_loop(0, C // 128, chunk, jnp.zeros((8, BW), F32))
            acc = jnp.sum(acc, axis=0, keepdims=True)
            for j in range(2):
                r = pl.ds(b * 2 + j, 1)
                rl[n, half, r, :] = acc[:, 256 * j:256 * j + 256] * fac[half, r, :]
            return 0

        lax.fori_loop(0, 4, row_block, 0)

    for n in range(2):
        mass_half(0)
        landed(second)
        if n == 0:
            start_weights(1)
        else:
            rw[1] = fac[1] / (TOTAL * summed(rl2[n, 1], rb.at[n, 1], 3))
        mass_half(1)
        for t in range(NZ):
            ml[n, t:t + 1, :] = jnp.sum(part[t * CH:(t + 1) * CH, :].T, axis=0, keepdims=True)
        landed(push(ml.at[n], mr.at[n], z_peers, m_s.at[n], m_r.at[n]))
        scale = 1.0 / (TOTAL * summed(ml[n], mr.at[n], 7))
        for t in range(NZ):
            scol[t * CH:(t + 1) * CH, :] = jnp.broadcast_to(scale[t:t + 1, :], (CH, CH)).T
        row_half(n + 1, 0)
        first = push_1(n + 1, 0)
        row_half(n + 1, 1)
        second = push_1(n + 1, 1)
        landed(first)
        rl2[n + 1, 0] = summed(rl[n + 1, 0], ra.at[n + 1, 0], 7)
        first = push_2(n + 1, 0)
        landed(second)
        rl2[n + 1, 1] = summed(rl[n + 1, 1], ra.at[n + 1, 1], 7)
        second = push_2(n + 1, 1)
        landed(first)
        rw[0] = fac[0] / (TOTAL * summed(rl2[n + 1, 0], rb.at[n + 1, 0], 3))

    ws = (w0, w1)

    def weigh(i, halfway=None):
        for j, q in enumerate(GROUPS[i]):
            t = (z + q + NZ) % NZ
            rows = pl.ds(pl.multiple_of(t * CH, CH), CH)
            acc = jnp.zeros((CH, 128), F32)
            for b in range(NB):
                if b == 4 and halfway is not None:
                    halfway()
                for l in range(BW // 128):
                    value = weighted(b, rows, l)
                    acc = acc + value
                    ws[i % 2][j * CH:(j + 1) * CH, b * BW + l * 128:b * BW + (l + 1) * 128] = value.astype(BF16)
            ml[2, pl.ds(t, 1), :] = jnp.sum(acc.T, axis=0, keepdims=True)

    def multiply(i):
        n = len(GROUPS[i])
        first = POS[GROUPS[i][0]]
        e = emb[...].reshape(NB * BW, D)
        num[first:first + n] = jnp.dot(
            ws[i % 2][0:n * CH, :], e, preferred_element_type=F32
        ).reshape(n, CH, D)

    rs = {}

    def hop(name, q, rows, before=None):
        sign = (1 if name[0] in ("RA", "RB") else -1)
        i = len(rs)
        value = num[POS[q], rows, :]
        if before is not None:
            rs[before].wait_recv()
            value = value + rcv[slot[before]].astype(F32)
        snd[i] = value.astype(BF16)
        slot[name] = i
        copy = pltpu.make_async_remote_copy(
            src_ref=snd.at[i], dst_ref=rcv.at[i], send_sem=rs_s.at[i], recv_sem=rs_r.at[i],
            device_id=at(dz=sign), device_id_type=MESH,
        )
        copy.start()
        rs[name] = copy

    slot = {}
    lo, hi = slice(0, 64), slice(64, 128)

    def last_weights():
        landed(second)
        rw[1] = fac[1] / (TOTAL * summed(rl2[2, 1], rb.at[2, 1], 3))

    weigh(0, last_weights)
    for i in range(5):
        multiply(i)
        if i < 4:
            weigh(i + 1)
        if i == 0:
            hop(("RB", 0), 4, lo)
            hop(("LB", 0), 4, hi)
        elif i == 1:
            hop(("RA", 1), 3, hi)
            hop(("LA", 1), -3, lo)
        elif i == 2:
            hop(("RB", 1), 3, lo, ("RB", 0))
            hop(("LB", 1), -3, hi, ("LB", 0))
        elif i == 3:
            hop(("RA", 2), 2, hi, ("RA", 1))
            hop(("LA", 2), -2, lo, ("LA", 1))
            last = push(ml.at[2], mr.at[2], z_peers, m_s.at[2], m_r.at[2])
    hop(("RB", 2), 2, lo, ("RB", 1))
    hop(("LB", 2), -2, hi, ("LB", 1))
    hop(("RA", 3), 1, hi, ("RA", 2))
    hop(("LA", 3), -1, lo, ("LA", 2))
    hop(("RB", 3), 1, lo, ("RB", 2))
    hop(("LB", 3), -1, hi, ("LB", 2))

    for copy in last:
        copy.wait_recv()
    mass = ml[2, pl.ds(z, 1), :]
    for k in range(7):
        mass = mass + mr[2, k, pl.ds(z, 1), :]
    column = jnp.broadcast_to(mass, (CH, CH)).T
    column = jnp.concatenate([column] * (D // CH), axis=1)
    for rows, one, two in ((hi, ("RA", 3), ("LB", 3)), (lo, ("LA", 3), ("RB", 3))):
        rs[one].wait_recv()
        rs[two].wait_recv()
        total = num[POS[0], rows, :] + rcv[slot[one]].astype(F32) + rcv[slot[two]].astype(F32)
        out_ref[rows, :] = (total / column[rows, :]).astype(BF16)

    for copy in list(ag.values()) + sent + list(rs.values()):
        copy.wait_send()


def local(embeddings, centroids):
    e = embeddings.reshape(16, PIECE, D)
    k = centroids.reshape(NZ, NY, CH, D)
    dma = pltpu.SemaphoreType.DMA
    v = pltpu.VMEM
    out = pl.pallas_call(
        body,
        out_shape=jax.ShapeDtypeStruct((CH, D), BF16),
        in_specs=[pl.BlockSpec(memory_space=pl.ANY)] * 2,
        out_specs=pl.BlockSpec(memory_space=pltpu.VMEM),
        scratch_shapes=[
            v((64, PIECE, D), BF16), v((NZ, CH, D), BF16), v((NB, C, BW), F32), v((C, BW), F32), v((C, BW), F32),
            v((2, 8, 256), F32), v((3, 2, 8, 256), F32), v((3, 2, 8, 256), F32),
            v((3, 2, 7, 8, 256), F32), v((3, 2, 3, 8, 256), F32),
            v((2, 8, 256), F32), v((2, 8, 256), F32), v((C, 128), F32), v((C, 128), F32),
            v((3, NZ, CH), F32), v((3, 7, NZ, CH), F32),
            v((2 * CH, NB * BW), BF16), v((2 * CH, NB * BW), BF16), v((NZ, CH, D), F32),
            v((14, 64, D), BF16), v((14, 64, D), BF16),
            dma((2,)), dma((48,)), dma((48,)), dma((3, 2, 7)), dma((3, 2, 7)), dma((3, 2, 3)), dma((3, 2, 3)),
            dma((3, 7)), dma((3, 7)), dma((14,)), dma((14,)),
        ],
        compiler_params=pltpu.CompilerParams(
            collective_id=0, has_side_effects=True, vmem_limit_bytes=60 * 1024 * 1024
        ),
        cost_estimate=pl.CostEstimate(
            flops=4 * C * NB * BW * D, bytes_accessed=8 * 1024 * 1024, transcendentals=C * NB * BW
        ),
    )(e, k)
    return out[None]


def solution(mesh):
    return jax.shard_map(
        local,
        mesh=mesh,
        in_specs=(P("docs", None), P("cent", None)),
        out_specs=P("cent", "docs", None),
        check_vma=False,
    )
```

time: 102 us -> 99.6 us (0.976)
  Pallas kernels: 99.2 us -> 97 us
    pallas_call x1, Pallas kernels: 99.2 us -> 97 us  [local(): pl.pallas_call(body, out_shape=jax.ShapeDtypeStruct((CH, D), BF16), in_sp...]
where the time goes in v2:
time: 99.6 us; the launch traced here: 98.6 us
  Pallas kernels  97 us (97%)
  local copies, waits for them, and re-layouts  1.62 us (2%)
    pallas_call x1, Pallas kernels, local(): pl.pallas_call(body, out_shape=jax.ShapeDtypeStruct((CH, D), BF16), in_sp...  97 us

profile of v2, /device:TPU:64, one launch (start us, length us, event | category | flops | bytes accessed | tf_op | source)
XLA Modules:
  0.0 98.6 jit_solution(10341104030207379467)
XLA Ops:
  0.0 97.0 %shard_map.28 = bf16[128,768]{1,0:T(8,128)(2,1)} custom-call(bf16[16,64,768]{2,1,0:T(8,128)(2,1)} %bitcast.5, bf16[8,4,128,768]{3,2,1,0:T(8,128)(2,1)} %bitcast.4), custom_call_target="tpu_custom_call" | custom-call | flops 12884901888 | bytes 8388608 | tf_op jit(solution)/shard_map/pallas_call | solution.py:424
  97.0 1.6 %copy.4 = bf16[1,128,768]{2,1,0:T(8,128)(2,1)} copy(bf16[1,128,768]{2,1,0:T(8,128)(2,1)} %bitcast.3) | data formatting | bytes 393216

commit v3 on v2

--- a/solution.py
+++ b/solution.py
@@ -19,7 +19,7 @@
 TOTAL = 32768.0
 EXP2_SCALE = 10.0 * float(np.log2(np.e))
 
-GROUPS = ((4,), (3, -3), (2, -2), (1, -1), (0,))
+GROUPS = ((4, 3), (-3, 2), (-2, 1), (-1, 0))
 POS = {q: i for i, q in enumerate(q for group in GROUPS for q in group)}
 LN2 = float(np.log(2.0))
 
@@ -59,110 +59,128 @@
 
     ag = {}
 
-    def send(name, where, target, src=None):
+    def plan(name, where, target, src=None):
         i = len(ag)
-        copy = pltpu.make_async_remote_copy(
+        ag[name] = pltpu.make_async_remote_copy(
             src_ref=emb.at[where] if src is None else src, dst_ref=emb.at[where],
             send_sem=ag_s.at[i], recv_sem=ag_r.at[i], device_id=target, device_id_type=MESH,
         )
-        copy.start()
-        ag[name] = copy
-
-    def send_own(name, h, dx, s):
-        send(name, piece(0, h, dx), at(dy=s), emb_hbm.at[h * 8 + ((x + dx + NX) % NX) * 2 + c])
+
+    def plan_own(name, h, dx, s):
+        plan(name, piece(0, h, dx), at(dy=s), emb_hbm.at[h * 8 + ((x + dx + NX) % NX) * 2 + c])
+
+    plan_own(("f", 1), 1, 0, 1)
+    plan_own(("f", -1), 0, 0, -1)
+    plan_own(("g", 1), 0, 0, 1)
+    plan_own(("g", -1), 1, 0, -1)
+    plan(("y3", 1), piece(-1, 1, 0), at(dy=1))
+    plan(("y3", -1), piece(1, 0, 0), at(dy=-1))
+    for k in (1, 2, -1):
+        for s in (1, -1):
+            plan_own(("k", s, k), 0, k, s)
+    for dy, h in ((-1, 1), (1, 1), (2, 0), (2, 1)):
+        for s in (1, -1):
+            plan(("x1", s, dy, h), piece(dy, h, 0), at(dx=s))
+    for s, dy, h in ((-1, -1, 1), (1, 1, 1), (1, 2, 0), (-1, 2, 1)):
+        plan(("x2", s, dy, h), piece(dy, h, -s), at(dx=s))
+    for dy in (-1, 1, 2):
+        for h in (0, 1):
+            for dx in (0, 1, 2, -1):
+                plan(("s", dy, h, dx), piece(dy, h, dx), at(flip=True))
+
+    def send(*names):
+        for name in names:
+            ag[name].start()
 
     def got(*names):
         for name in names:
             ag[name].wait_recv()
 
     def to_sibling(*pieces):
-        for dy, h, dx in pieces:
-            send(("s", dy, h, dx), piece(dy, h, dx), at(flip=True))
-
-    def to_x(*pieces):
-        for s, dy, h in pieces:
-            send(("x1", s, dy, h), piece(dy, h, 0), at(dx=s))
+        send(*[("s", *p) for p in pieces])
 
     def block_ready(dy, h):
-        for dx in (0, 1, 2, -1):
-            got(("s", dy, h, dx))
-
-    send_own(("f", 1), 1, 0, 1)
-    send_own(("f", -1), 0, 0, -1)
-    send_own(("g", 1), 0, 0, 1)
-    send_own(("g", -1), 1, 0, -1)
+        got(*[("s", dy, h, dx) for dx in (0, 1, 2, -1)])
+
+    send(("f", 1), ("f", -1), ("g", 1), ("g", -1))
     load_e.wait()
     load_c.wait()
 
     def phase_a():
         got(("f", 1), ("f", -1))
-        to_x((1, -1, 1), (-1, -1, 1))
-        send(("y3", 1), piece(-1, 1, 0), at(dy=1))
-        send(("y3", -1), piece(1, 0, 0), at(dy=-1))
-        for k in (1, 2, -1):
-            for s in (1, -1):
-                send_own(("k", s, k), 0, k, s)
+        send(("x1", 1, -1, 1), ("x1", -1, -1, 1), ("y3", 1), ("y3", -1))
+        send(*[("k", s, k) for k in (1, 2, -1) for s in (1, -1)])
         to_sibling((-1, 1, 0), (1, 0, 0))
 
-    def phase_b():
+    def phase_c():
         got(("g", 1), ("g", -1))
-        to_x((1, 1, 1), (-1, 1, 1))
+        send(("x1", 1, 1, 1), ("x1", -1, 1, 1))
         to_sibling((-1, 0, 0), (1, 1, 0))
-
-    def phase_c():
         got(("x1", -1, -1, 1), ("x1", 1, -1, 1))
-        send(("x2", -1, -1, 1), piece(-1, 1, 1), at(dx=-1))
+        send(("x2", -1, -1, 1))
         to_sibling((-1, 1, 1), (-1, 1, -1))
         got(("x1", 1, 1, 1), ("x1", -1, 1, 1))
-        send(("x2", 1, 1, 1), piece(1, 1, -1), at(dx=1))
+        send(("x2", 1, 1, 1))
         to_sibling((1, 1, -1), (1, 1, 1))
         got(("y3", 1), ("y3", -1))
-        to_x((1, 2, 0), (-1, 2, 1), (1, 2, 1), (-1, 2, 0))
+        send(("x1", 1, 2, 0), ("x1", -1, 2, 1), ("x1", 1, 2, 1), ("x1", -1, 2, 0))
         to_sibling((2, 1, 0), (2, 0, 0))
         got(("x2", 1, 1, 1), ("x2", -1, -1, 1))
         to_sibling((1, 1, 2), (-1, 1, 2))
+        block_ready(1, 1)
 
     def phase_f():
         for k in (1, 2):
             got(("k", 1, k), ("k", -1, k))
             to_sibling((1, 0, k), (-1, 0, k))
+        block_ready(-1, 1)
 
     def phase_g():
         got(("x1", 1, 2, 0), ("x1", -1, 2, 1))
-        send(("x2", 1, 2, 0), piece(2, 0, -1), at(dx=1))
-        send(("x2", -1, 2, 1), piece(2, 1, 1), at(dx=-1))
+        send(("x2", 1, 2, 0), ("x2", -1, 2, 1))
         to_sibling((2, 0, -1), (2, 1, 1))
         got(("k", 1, -1), ("k", -1, -1))
         to_sibling((1, 0, -1), (-1, 0, -1))
+        block_ready(1, 0)
 
     def phase_h():
         got(("x1", 1, 2, 1), ("x1", -1, 2, 0))
         to_sibling((2, 1, -1), (2, 0, 1))
+        block_ready(-1, 0)
 
     def phase_i():
         got(("x2", 1, 2, 0), ("x2", -1, 2, 1))
         to_sibling((2, 0, 2), (2, 1, 2))
+        block_ready(2, 0)
+
+    def phase_j():
+        block_ready(2, 1)
 
     sent = []
 
-    def push(src, dst, peers, ssem, rsem):
+    def push(src, dst, peers, ssem, rsem, start=True):
         copies = []
         for k, peer in enumerate(peers):
             copy = pltpu.make_async_remote_copy(
                 src_ref=src, dst_ref=dst.at[k], send_sem=ssem.at[k], recv_sem=rsem.at[k],
                 device_id=peer, device_id_type=MESH,
             )
-            copy.start()
             copies.append(copy)
         sent.extend(copies)
+        if start:
+            begin(copies)
         return copies
+
+    def begin(copies):
+        for copy in copies:
+            copy.start()
 
     def landed(copies):
         for copy in copies:
             copy.wait_recv()
 
-    def push_1(n, half):
-        return push(rl.at[n, half], ra.at[n, half], cent_peers, r1_s.at[n, half], r1_r.at[n, half])
+    def push_1(n, half, start=True):
+        return push(rl.at[n, half], ra.at[n, half], cent_peers, r1_s.at[n, half], r1_r.at[n, half], start)
 
     def push_2(n, half):
         return push(rl2.at[n, half], rb.at[n, half], y_peers, r2_s.at[n, half], r2_r.at[n, half])
@@ -182,21 +200,18 @@
             total = total + jnp.exp2(others[k] - top)
         return top + jnp.log(total) * (1.0 / LN2)
 
-    def block_at(dy, h):
-        return ((y + dy + NY) % NY) * 2 + h
-
-    blocks = ((0, 0), (0, 1), (1, 1), (-1, 1), (1, 0), (-1, 0), (2, 0), (2, 1))
-    bufs = (buf0, buf1)
-    highs = {}
-
-    def step(new, old):
-        if old is not None:
-            top = jnp.max(highs[old], axis=0, keepdims=True)
-            total = jnp.zeros((8, BW), F32)
-            old_buf, place = bufs[old % 2], block_at(*blocks[old])
+    def place_of(p, odd):
+        d = (p + 1) // 2
+        if odd:
+            return ((y - d + NY) % NY) * 2 + 1 - (1 - p % 2) * (p // 2)
+        return ((y + d) % NY) * 2 + (p % 2) * (1 - p // 2)
+
+    def step(new_buf, new, old_buf, old, old_max, half, row):
+        top = jnp.max(old_max, axis=0, keepdims=True)
+        total = jnp.zeros((8, BW), F32)
+        new_max = None
         if new is not None:
-            e = emb[pl.ds(block_at(*blocks[new]) * 8, 8)].reshape(BW, D)
-            new_buf, new_max = bufs[new % 2], None
+            e = emb[pl.ds(new * 8, 8)].reshape(BW, D)
         for i in range(4):
             rows = slice(256 * i, 256 * i + 256)
             if new is not None:
@@ -207,51 +222,45 @@
                 new_buf[rows, :] = raw
                 high = jnp.max(raw.reshape(32, 8, BW), axis=0)
                 new_max = high if new_max is None else jnp.maximum(new_max, high)
-            if old is not None:
-                value = jnp.exp2((old_buf[rows, :] - top) * EXP2_SCALE)
-                kern[place, rows, :] = value
-                total = total + jnp.sum(value.reshape(32, 8, BW), axis=0)
-        if new is not None:
-            highs[new] = new_max
-        if old is not None:
-            scaled = top * EXP2_SCALE
-            whole = scaled + jnp.log(jnp.sum(total, axis=0, keepdims=True)) * (1.0 / LN2)
-            for j in range(2):
-                lanes = slice(256 * j, 256 * j + 256)
-                r = (old % 4) * 2 + j
-                rl[0, old // 4, r:r + 1, :] = whole[:, lanes]
-                top_of[place // 4, pl.ds((place % 4) * 2 + j, 1), :] = scaled[:, lanes]
-
-    step(0, None)
-    phase_a()
-    step(1, 0)
-    phase_b()
-    step(None, 1)
-    phase_c()
-    block_ready(*blocks[2])
-    step(2, None)
-    phase_f()
-    block_ready(*blocks[3])
-    step(3, 2)
-    phase_g()
-    block_ready(*blocks[4])
-    step(4, 3)
-    first = push_1(0, 0)
-    phase_h()
-    block_ready(*blocks[5])
-    step(5, 4)
-    phase_i()
-    block_ready(*blocks[6])
-    step(6, 5)
-    block_ready(*blocks[7])
-    step(7, 6)
-    step(None, 7)
+            value = jnp.exp2((old_buf[rows, :] - top) * EXP2_SCALE)
+            kern[old, rows, :] = value
+            total = total + jnp.sum(value.reshape(32, 8, BW), axis=0)
+        scaled = top * EXP2_SCALE
+        whole = scaled + jnp.log(jnp.sum(total, axis=0, keepdims=True)) * (1.0 / LN2)
+        for j in range(2):
+            lanes = slice(256 * j, 256 * j + 256)
+            rl[0, half, pl.ds(row + j, 1), :] = whole[:, lanes]
+            top_of[old // 4, pl.ds((old % 4) * 2 + j, 1), :] = scaled[:, lanes]
+        return new_max
+
+    first = push_1(0, 0, start=False)
+
+    def two_steps(p, high):
+        pl.when(p == 1)(phase_c)
+        pl.when(p == 2)(phase_g)
+        pl.when(p == 3)(phase_i)
+        q = (p + 3) % 4
+        high = step(buf0, place_of(p, False), buf1, place_of(q, True), high, q // 2, (q % 2) * 4 + 2)
+        pl.when(p == 0)(phase_a)
+        pl.when(p == 1)(phase_f)
+
+        @pl.when(p == 2)
+        def _():
+            begin(first)
+            phase_h()
+
+        pl.when(p == 3)(phase_j)
+        return step(buf1, place_of(p, True), buf0, place_of(p, False), high, p // 2, (p % 2) * 4)
+
+    buf1[...] = jnp.zeros((C, BW), F32)
+    high = lax.fori_loop(0, 4, two_steps, jnp.zeros((8, BW), F32))
+    step(None, None, buf1, place_of(3, True), high, 1, 6)
     second = push_1(0, 1)
     for half, copies in ((0, first), (1, second)):
         landed(copies)
         merged = log_summed(rl[0, half], ra.at[0, half], 7)
         for j in range(8):
-            place = block_at(*blocks[4 * half + j // 2])
+            place = place_of(2 * half + j // 4, j // 2 % 2 == 1)
             rl2[0, place // 4, pl.ds((place % 4) * 2 + j % 2, 1), :] = merged[j:j + 1, :]
     first, second = push_2(0, 0), push_2(0, 1)
 
@@ -325,29 +334,41 @@
         landed(first)
         rw[0] = fac[0] / (TOTAL * summed(rl2[n + 1, 0], rb.at[n + 1, 0], 3))
 
-    ws = (w0, w1)
-
-    def weigh(i, halfway=None):
+    def chunk_at(q):
+        return (z + q + NZ) % NZ
+
+    def weigh(w, i, b):
+        ws = [rw[b // 4, pl.ds((b % 4) * 2 + j, 1), :] for j in range(2)]
         for j, q in enumerate(GROUPS[i]):
-            t = (z + q + NZ) % NZ
-            rows = pl.ds(pl.multiple_of(t * CH, CH), CH)
-            acc = jnp.zeros((CH, 128), F32)
-            for b in range(NB):
-                if b == 4 and halfway is not None:
-                    halfway()
-                for l in range(BW // 128):
-                    value = weighted(b, rows, l)
-                    acc = acc + value
-                    ws[i % 2][j * CH:(j + 1) * CH, b * BW + l * 128:b * BW + (l + 1) * 128] = value.astype(BF16)
-            ml[2, pl.ds(t, 1), :] = jnp.sum(acc.T, axis=0, keepdims=True)
-
-    def multiply(i):
-        n = len(GROUPS[i])
-        first = POS[GROUPS[i][0]]
-        e = emb[...].reshape(NB * BW, D)
-        num[first:first + n] = jnp.dot(
-            ws[i % 2][0:n * CH, :], e, preferred_element_type=F32
-        ).reshape(n, CH, D)
+            rows = pl.ds(pl.multiple_of(chunk_at(q) * CH, CH), CH)
+            place = slice((2 * i + j) * CH, (2 * i + j + 1) * CH)
+            acc = part[place, :]
+            for l in range(BW // 128):
+                value = kern[b, rows, l * 128:l * 128 + 128] * ws[l // 2][:, (l % 2) * 128:(l % 2) * 128 + 128]
+                acc = acc + value
+                w[j * CH:(j + 1) * CH, l * 128:(l + 1) * 128] = value.astype(BF16)
+            part[place, :] = acc
+
+    def multiply(w, i, b):
+        e = emb[pl.ds(b * 8, 8)].reshape(BW, D)
+        num[2 * i:2 * i + 2] += jnp.dot(w[...], e, preferred_element_type=F32).reshape(2, CH, D)
+
+    def group(i):
+        num[2 * i:2 * i + 2] = jnp.zeros((2, CH, D), F32)
+
+        def two(k, _):
+            weigh(w1, i, 2 * k + 1)
+            multiply(w0, i, 2 * k)
+            weigh(w0, i, 2 * k + 2)
+            multiply(w1, i, 2 * k + 1)
+            return 0
+
+        lax.fori_loop(0, 3, two, 0)
+        weigh(w1, i, 7)
+        multiply(w0, i, 6)
+        if i < 3:
+            weigh(w0, i + 1, 0)
+        multiply(w1, i, 7)
 
     rs = {}
 
@@ -370,28 +391,26 @@
     slot = {}
     lo, hi = slice(0, 64), slice(64, 128)
 
-    def last_weights():
-        landed(second)
-        rw[1] = fac[1] / (TOTAL * summed(rl2[2, 1], rb.at[2, 1], 3))
-
-    weigh(0, last_weights)
-    for i in range(5):
-        multiply(i)
-        if i < 4:
-            weigh(i + 1)
+    part[...] = jnp.zeros((C, 128), F32)
+    weigh(w0, 0, 0)
+    landed(second)
+    rw[1] = fac[1] / (TOTAL * summed(rl2[2, 1], rb.at[2, 1], 3))
+    for i in range(4):
+        group(i)
         if i == 0:
             hop(("RB", 0), 4, lo)
             hop(("LB", 0), 4, hi)
+            hop(("RA", 1), 3, hi)
         elif i == 1:
-            hop(("RA", 1), 3, hi)
             hop(("LA", 1), -3, lo)
         elif i == 2:
             hop(("RB", 1), 3, lo, ("RB", 0))
             hop(("LB", 1), -3, hi, ("LB", 0))
-        elif i == 3:
-            hop(("RA", 2), 2, hi, ("RA", 1))
-            hop(("LA", 2), -2, lo, ("LA", 1))
-            last = push(ml.at[2], mr.at[2], z_peers, m_s.at[2], m_r.at[2])
+    for j, q in enumerate(q for g in GROUPS for q in g):
+        ml[2, pl.ds(chunk_at(q), 1), :] = jnp.sum(part[j * CH:(j + 1) * CH, :].T, axis=0, keepdims=True)
+    last = push(ml.at[2], mr.at[2], z_peers, m_s.at[2], m_r.at[2])
+    hop(("RA", 2), 2, hi, ("RA", 1))
+    hop(("LA", 2), -2, lo, ("LA", 1))
     hop(("RB", 2), 2, lo, ("RB", 1))
     hop(("LB", 2), -2, hi, ("LB", 1))
     hop(("RA", 3), 1, hi, ("RA", 2))
@@ -432,7 +451,7 @@
             v((3, 2, 7, 8, 256), F32), v((3, 2, 3, 8, 256), F32),
             v((2, 8, 256), F32), v((2, 8, 256), F32), v((C, 128), F32), v((C, 128), F32),
             v((3, NZ, CH), F32), v((3, 7, NZ, CH), F32),
-            v((2 * CH, NB * BW), BF16), v((2 * CH, NB * BW), BF16), v((NZ, CH, D), F32),
+            v((2 * CH, BW), BF16), v((2 * CH, BW), BF16), v((NZ, CH, D), F32),
             v((14, 64, D), BF16), v((14, 64, D), BF16),
             dma((2,)), dma((48,)), dma((48,)), dma((3, 2, 7)), dma((3, 2, 7)), dma((3, 2, 3)), dma((3, 2, 3)),
             dma((3, 7)), dma((3, 7)), dma((14,)), dma((14,)),

time: 99.6 us -> 99.9 us (level)
  no operation moved by 1% of the time
where the time goes in v3:
time: 99.9 us; the launch traced here: 98.8 us
  Pallas kernels  97.2 us (97%)
  local copies, waits for them, and re-layouts  1.62 us (2%)
    pallas_call x1, Pallas kernels, local(): pl.pallas_call(body, out_shape=jax.ShapeDtypeStruct((CH, D), BF16), in_sp...  97.2 us

profile of v3, /device:TPU:64, one launch (start us, length us, event | category | flops | bytes accessed | tf_op | source)
XLA Modules:
  0.0 98.8 jit_solution(7531557040275922851)
XLA Ops:
  0.0 97.2 %shard_map.28 = bf16[128,768]{1,0:T(8,128)(2,1)} custom-call(bf16[16,64,768]{2,1,0:T(8,128)(2,1)} %bitcast.5, bf16[8,4,128,768]{3,2,1,0:T(8,128)(2,1)} %bitcast.4), custom_call_target="tpu_custom_call" | custom-call | flops 12884901888 | bytes 8388608 | tf_op jit(solution)/shard_map/pallas_call | solution.py:443
  97.2 1.6 %copy.4 = bf16[1,128,768]{2,1,0:T(8,128)(2,1)} copy(bf16[1,128,768]{2,1,0:T(8,128)(2,1)} %bitcast.3) | data formatting | bytes 393216

commit v4 on v3

--- a/solution.py
+++ b/solution.py
@@ -19,7 +19,8 @@
 TOTAL = 32768.0
 EXP2_SCALE = 10.0 * float(np.log2(np.e))
 
-GROUPS = ((4, 3), (-3, 2), (-2, 1), (-1, 0))
+GROUPS = ((4, 3, -3, 2), (-2, 1, -1, 0))
+GROUP = len(GROUPS[0])
 POS = {q: i for i, q in enumerate(q for group in GROUPS for q in group)}
 LN2 = float(np.log(2.0))
 
@@ -209,22 +210,23 @@
     def step(new_buf, new, old_buf, old, old_max, half, row):
         top = jnp.max(old_max, axis=0, keepdims=True)
         total = jnp.zeros((8, BW), F32)
-        new_max = None
+        new_max = []
         if new is not None:
             e = emb[pl.ds(new * 8, 8)].reshape(BW, D)
         for i in range(4):
             rows = slice(256 * i, 256 * i + 256)
-            if new is not None:
+            if new is not None and i % 2 == 0:
+                lanes = slice(128 * i, 128 * i + 256)
                 raw = lax.dot_general(
-                    cen[2 * i:2 * i + 2].reshape(256, D), e, (((1,), (1,)), ((), ())),
-                    preferred_element_type=F32,
+                    cen[...].reshape(C, D), e[lanes, :], (((1,), (1,)), ((), ())), preferred_element_type=F32
                 )
-                new_buf[rows, :] = raw
-                high = jnp.max(raw.reshape(32, 8, BW), axis=0)
-                new_max = high if new_max is None else jnp.maximum(new_max, high)
+                new_buf[:, lanes] = raw
+                new_max.append(jnp.max(raw.reshape(C // 8, 8, 256), axis=0))
             value = jnp.exp2((old_buf[rows, :] - top) * EXP2_SCALE)
             kern[old, rows, :] = value
             total = total + jnp.sum(value.reshape(32, 8, BW), axis=0)
+        if new is not None:
+            new_max = jnp.concatenate(new_max, axis=1)
         scaled = top * EXP2_SCALE
         whole = scaled + jnp.log(jnp.sum(total, axis=0, keepdims=True)) * (1.0 / LN2)
         for j in range(2):
@@ -341,7 +343,7 @@
         ws = [rw[b // 4, pl.ds((b % 4) * 2 + j, 1), :] for j in range(2)]
         for j, q in enumerate(GROUPS[i]):
             rows = pl.ds(pl.multiple_of(chunk_at(q) * CH, CH), CH)
-            place = slice((2 * i + j) * CH, (2 * i + j + 1) * CH)
+            place = slice((GROUP * i + j) * CH, (GROUP * i + j + 1) * CH)
             acc = part[place, :]
             for l in range(BW // 128):
                 value = kern[b, rows, l * 128:l * 128 + 128] * ws[l // 2][:, (l % 2) * 128:(l % 2) * 128 + 128]
@@ -351,11 +353,9 @@
 
     def multiply(w, i, b):
         e = emb[pl.ds(b * 8, 8)].reshape(BW, D)
-        num[2 * i:2 * i + 2] += jnp.dot(w[...], e, preferred_element_type=F32).reshape(2, CH, D)
-
-    def group(i):
-        num[2 * i:2 * i + 2] = jnp.zeros((2, CH, D), F32)
-
+        num[GROUP * i:GROUP * i + GROUP] += jnp.dot(w[...], e, preferred_element_type=F32).reshape(GROUP, CH, D)
+
+    def group(i, start, stop):
         def two(k, _):
             weigh(w1, i, 2 * k + 1)
             multiply(w0, i, 2 * k)
@@ -363,10 +363,12 @@
             multiply(w1, i, 2 * k + 1)
             return 0
 
-        lax.fori_loop(0, 3, two, 0)
+        lax.fori_loop(start, stop, two, 0)
+
+    def group_end(i):
         weigh(w1, i, 7)
         multiply(w0, i, 6)
-        if i < 3:
+        if i == 0:
             weigh(w0, i + 1, 0)
         multiply(w1, i, 7)
 
@@ -395,17 +397,18 @@
     weigh(w0, 0, 0)
     landed(second)
     rw[1] = fac[1] / (TOTAL * summed(rl2[2, 1], rb.at[2, 1], 3))
-    for i in range(4):
-        group(i)
-        if i == 0:
-            hop(("RB", 0), 4, lo)
-            hop(("LB", 0), 4, hi)
-            hop(("RA", 1), 3, hi)
-        elif i == 1:
-            hop(("LA", 1), -3, lo)
-        elif i == 2:
-            hop(("RB", 1), 3, lo, ("RB", 0))
-            hop(("LB", 1), -3, hi, ("LB", 0))
+    num[...] = jnp.zeros((NZ, CH, D), F32)
+    group(0, 0, 3)
+    group_end(0)
+    hop(("RB", 0), 4, lo)
+    hop(("LB", 0), 4, hi)
+    hop(("RA", 1), 3, hi)
+    hop(("LA", 1), -3, lo)
+    group(1, 0, 2)
+    hop(("RB", 1), 3, lo, ("RB", 0))
+    hop(("LB", 1), -3, hi, ("LB", 0))
+    group(1, 2, 3)
+    group_end(1)
     for j, q in enumerate(q for g in GROUPS for q in g):
         ml[2, pl.ds(chunk_at(q), 1), :] = jnp.sum(part[j * CH:(j + 1) * CH, :].T, axis=0, keepdims=True)
     last = push(ml.at[2], mr.at[2], z_peers, m_s.at[2], m_r.at[2])
@@ -451,7 +454,7 @@
             v((3, 2, 7, 8, 256), F32), v((3, 2, 3, 8, 256), F32),
             v((2, 8, 256), F32), v((2, 8, 256), F32), v((C, 128), F32), v((C, 128), F32),
             v((3, NZ, CH), F32), v((3, 7, NZ, CH), F32),
-            v((2 * CH, BW), BF16), v((2 * CH, BW), BF16), v((NZ, CH, D), F32),
+            v((GROUP * CH, BW), BF16), v((GROUP * CH, BW), BF16), v((NZ, CH, D), F32),
             v((14, 64, D), BF16), v((14, 64, D), BF16),
             dma((2,)), dma((48,)), dma((48,)), dma((3, 2, 7)), dma((3, 2, 7)), dma((3, 2, 3)), dma((3, 2, 3)),
             dma((3, 7)), dma((3, 7)), dma((14,)), dma((14,)),

time: 99.9 us -> 101 us (1.011)
  Pallas kernels: 97.2 us -> 98.6 us
    pallas_call x1, Pallas kernels: 97.2 us -> 98.6 us  [local(): pl.pallas_call(body, out_shape=jax.ShapeDtypeStruct((CH, D), BF16), in_sp...]
where the time goes in v4:
time: 101 us; the launch traced here: 100 us
  Pallas kernels  98.6 us (98%)
  local copies, waits for them, and re-layouts  1.62 us (2%)
    pallas_call x1, Pallas kernels, local(): pl.pallas_call(body, out_shape=jax.ShapeDtypeStruct((CH, D), BF16), in_sp...  98.6 us

profile of v4, /device:TPU:64, one launch (start us, length us, event | category | flops | bytes accessed | tf_op | source)
XLA Modules:
  0.0 100.3 jit_solution(15735157810714379623)
XLA Ops:
  0.0 98.6 %shard_map.28 = bf16[128,768]{1,0:T(8,128)(2,1)} custom-call(bf16[16,64,768]{2,1,0:T(8,128)(2,1)} %bitcast.5, bf16[8,4,128,768]{3,2,1,0:T(8,128)(2,1)} %bitcast.4), custom_call_target="tpu_custom_call" | custom-call | flops 12884901888 | bytes 8388608 | tf_op jit(solution)/shard_map/pallas_call | solution.py:446
  98.6 1.6 %copy.4 = bf16[1,128,768]{2,1,0:T(8,128)(2,1)} copy(bf16[1,128,768]{2,1,0:T(8,128)(2,1)} %bitcast.3) | data formatting | bytes 393216

commit v5 on v4

--- a/solution.py
+++ b/solution.py
@@ -28,7 +28,7 @@
 def body(
     emb_hbm, cen_hbm, out_ref,
     emb, cen, kern, buf0, buf1,
-    top_of, rl, rl2, ra, rb, fac, rw, part, scol, ml, mr, w0, w1, num, snd, rcv,
+    top_of, rl, rl2, ra, rb, fac, rw, part, scol, col, ml, mr, w0, w1, num, snd, rcv,
     ld_sem, ag_s, ag_r, r1_s, r1_r, r2_s, r2_r, m_s, m_r, rs_s, rs_r,
 ):
     docs = lax.axis_index("docs")
@@ -214,7 +214,6 @@
         if new is not None:
             e = emb[pl.ds(new * 8, 8)].reshape(BW, D)
         for i in range(4):
-            rows = slice(256 * i, 256 * i + 256)
             if new is not None and i % 2 == 0:
                 lanes = slice(128 * i, 128 * i + 256)
                 raw = lax.dot_general(
@@ -222,9 +221,11 @@
                 )
                 new_buf[:, lanes] = raw
                 new_max.append(jnp.max(raw.reshape(C // 8, 8, 256), axis=0))
-            value = jnp.exp2((old_buf[rows, :] - top) * EXP2_SCALE)
-            kern[old, rows, :] = value
-            total = total + jnp.sum(value.reshape(32, 8, BW), axis=0)
+            for k in range(4):
+                rows = slice(256 * i + 64 * k, 256 * i + 64 * k + 64)
+                value = jnp.exp2((old_buf[rows, :] - top) * EXP2_SCALE)
+                kern[old, rows, :] = value
+                total = total + jnp.sum(value.reshape(8, 8, BW), axis=0)
         if new is not None:
             new_max = jnp.concatenate(new_max, axis=1)
         scaled = top * EXP2_SCALE
@@ -275,40 +276,51 @@
     landed(first)
     start_weights(0)
 
-    def weighted(b, rows, l):
-        r = (b % 4) * 2 + l // 2
-        w = rw[b // 4, r:r + 1, (l % 2) * 128:(l % 2) * 128 + 128]
-        return kern[b, rows, l * 128:l * 128 + 128] * w
+    lane = lax.broadcasted_iota(jnp.int32, (8, 128), 1)
 
     def mass_half(half):
-        def chunk(g, _):
-            rows = pl.ds(pl.multiple_of(g * 64, 64), 64)
-            acc = jnp.zeros((64, 128), F32) if half == 0 else part[rows, :]
+        def chunk(t, _):
+            def tile(i):
+                return pl.ds(pl.multiple_of(t * CH + 8 * i, 8), 8)
+
+            acc = [None if half == 0 else part[tile(i), :] for i in range(16)]
             for b in range(4 * half, 4 * half + 4):
-                for l in range(BW // 128):
-                    acc = acc + weighted(b, rows, l)
-            part[rows, :] = acc
+                for l in range(4):
+                    r = (b % 4) * 2 + l // 2
+                    w = jnp.broadcast_to(rw[half, r:r + 1, (l % 2) * 128:(l % 2) * 128 + 128], (8, 128))
+                    for i in range(16):
+                        value = kern[b, tile(i), l * 128:l * 128 + 128] * w
+                        acc[i] = value if acc[i] is None else acc[i] + value
+            for i in range(16):
+                if half == 0:
+                    part[tile(i), :] = acc[i]
+                else:
+                    total = jnp.sum(acc[i], axis=1, keepdims=True)
+                    rows = slice(8 * i, 8 * i + 8)
+                    col[rows, :] = jnp.where(lane == t, total, col[rows, :])
             return 0
 
-        lax.fori_loop(0, C // 64, chunk, 0)
+        lax.fori_loop(0, NZ, chunk, 0)
 
     def row_half(n, half):
-        def row_block(b, _):
-            def chunk(g, acc):
-                rows = pl.ds(pl.multiple_of(g * 128, 128), 128)
-                s = scol[rows, :]
-                value = kern[4 * half + b, rows, :] * jnp.concatenate([s] * (BW // 128), axis=1)
-                return acc + jnp.sum(value.reshape(16, 8, BW), axis=0)
-
-            acc = lax.fori_loop(0, C // 128, chunk, jnp.zeros((8, BW), F32))
-            acc = jnp.sum(acc, axis=0, keepdims=True)
-            for j in range(2):
-                r = pl.ds(b * 2 + j, 1)
-                rl[n, half, r, :] = acc[:, 256 * j:256 * j + 256] * fac[half, r, :]
-            return 0
-
-        lax.fori_loop(0, 4, row_block, 0)
-
+        def chunk(t, acc):
+            acc = list(acc)
+            for i in range(16):
+                tile = pl.ds(pl.multiple_of(t * CH + 8 * i, 8), 8)
+                s = scol[tile, :]
+                for b in range(4):
+                    for l in range(4):
+                        acc[4 * b + l] += kern[4 * half + b, tile, l * 128:l * 128 + 128] * s
+            return tuple(acc)
+
+        acc = lax.fori_loop(0, NZ, chunk, tuple(jnp.zeros((8, 128), F32) for _ in range(16)))
+        for b in range(4):
+            for l in range(4):
+                r, lanes = b * 2 + l // 2, slice((l % 2) * 128, (l % 2) * 128 + 128)
+                total = jnp.sum(acc[4 * b + l], axis=0, keepdims=True)
+                rl[n, half, r:r + 1, lanes] = total * fac[half, r:r + 1, lanes]
+
+    col[...] = jnp.zeros((CH, CH), F32)
     for n in range(2):
         mass_half(0)
         landed(second)
@@ -317,12 +329,12 @@
         else:
             rw[1] = fac[1] / (TOTAL * summed(rl2[n, 1], rb.at[n, 1], 3))
         mass_half(1)
-        for t in range(NZ):
-            ml[n, t:t + 1, :] = jnp.sum(part[t * CH:(t + 1) * CH, :].T, axis=0, keepdims=True)
+        ml[n] = col[...].T[0:NZ, :]
         landed(push(ml.at[n], mr.at[n], z_peers, m_s.at[n], m_r.at[n]))
         scale = 1.0 / (TOTAL * summed(ml[n], mr.at[n], 7))
+        columns = jnp.concatenate([scale, jnp.zeros((CH - NZ, CH), F32)], axis=0).T
         for t in range(NZ):
-            scol[t * CH:(t + 1) * CH, :] = jnp.broadcast_to(scale[t:t + 1, :], (CH, CH)).T
+            scol[t * CH:(t + 1) * CH, :] = jnp.broadcast_to(columns[:, t:t + 1], (CH, CH))
         row_half(n + 1, 0)
         first = push_1(n + 1, 0)
         row_half(n + 1, 1)
@@ -410,7 +422,11 @@
     group(1, 2, 3)
     group_end(1)
     for j, q in enumerate(q for g in GROUPS for q in g):
-        ml[2, pl.ds(chunk_at(q), 1), :] = jnp.sum(part[j * CH:(j + 1) * CH, :].T, axis=0, keepdims=True)
+        for i in range(16):
+            rows = slice(8 * i, 8 * i + 8)
+            total = jnp.sum(part[j * CH + 8 * i:j * CH + 8 * i + 8, :], axis=1, keepdims=True)
+            col[rows, :] = jnp.where(lane == chunk_at(q), total, col[rows, :])
+    ml[2] = col[...].T[0:NZ, :]
     last = push(ml.at[2], mr.at[2], z_peers, m_s.at[2], m_r.at[2])
     hop(("RA", 2), 2, hi, ("RA", 1))
     hop(("LA", 2), -2, lo, ("LA", 1))
@@ -452,7 +468,7 @@
             v((64, PIECE, D), BF16), v((NZ, CH, D), BF16), v((NB, C, BW), F32), v((C, BW), F32), v((C, BW), F32),
             v((2, 8, 256), F32), v((3, 2, 8, 256), F32), v((3, 2, 8, 256), F32),
             v((3, 2, 7, 8, 256), F32), v((3, 2, 3, 8, 256), F32),
-            v((2, 8, 256), F32), v((2, 8, 256), F32), v((C, 128), F32), v((C, 128), F32),
+            v((2, 8, 256), F32), v((2, 8, 256), F32), v((C, 128), F32), v((C, 128), F32), v((CH, CH), F32),
             v((3, NZ, CH), F32), v((3, 7, NZ, CH), F32),
             v((GROUP * CH, BW), BF16), v((GROUP * CH, BW), BF16), v((NZ, CH, D), F32),
             v((14, 64, D), BF16), v((14, 64, D), BF16),

time: 101 us -> 101 us (level)
  no operation moved by 1% of the time
where the time goes in v5:
time: 101 us; the launch traced here: 99.6 us
  Pallas kernels  98 us (97%)
  local copies, waits for them, and re-layouts  1.62 us (2%)
    pallas_call x1, Pallas kernels, local(): pl.pallas_call(body, out_shape=jax.ShapeDtypeStruct((CH, D), BF16), in_sp...  98 us

profile of v5, /device:TPU:64, one launch (start us, length us, event | category | flops | bytes accessed | tf_op | source)
XLA Modules:
  0.0 99.6 jit_solution(6204290817433136926)
XLA Ops:
  0.0 98.0 %shard_map.28 = bf16[128,768]{1,0:T(8,128)(2,1)} custom-call(bf16[16,64,768]{2,1,0:T(8,128)(2,1)} %bitcast.5, bf16[8,4,128,768]{3,2,1,0:T(8,128)(2,1)} %bitcast.4), custom_call_target="tpu_custom_call" | custom-call | flops 12884901888 | bytes 8388608 | tf_op jit(solution)/shard_map/pallas_call | solution.py:462
  98.0 1.6 %copy.4 = bf16[1,128,768]{2,1,0:T(8,128)(2,1)} copy(bf16[1,128,768]{2,1,0:T(8,128)(2,1)} %bitcast.3) | data formatting | bytes 393216

commit v6 on v5

--- a/solution.py
+++ b/solution.py
@@ -19,7 +19,7 @@
 TOTAL = 32768.0
 EXP2_SCALE = 10.0 * float(np.log2(np.e))
 
-GROUPS = ((4, 3, -3, 2), (-2, 1, -1, 0))
+GROUPS = ((4, 3), (-3, 2), (-2, 1), (-1, 0))
 GROUP = len(GROUPS[0])
 POS = {q: i for i, q in enumerate(q for group in GROUPS for q in group)}
 LN2 = float(np.log(2.0))
@@ -179,6 +179,10 @@
     def landed(copies):
         for copy in copies:
             copy.wait_recv()
+
+    def drain(copies):
+        for copy in copies:
+            copy.wait_send()
 
     def push_1(n, half, start=True):
         return push(rl.at[n, half], ra.at[n, half], cent_peers, r1_s.at[n, half], r1_r.at[n, half], start)
@@ -259,6 +263,7 @@
     high = lax.fori_loop(0, 4, two_steps, jnp.zeros((8, BW), F32))
     step(None, None, buf1, place_of(3, True), high, 1, 6)
     second = push_1(0, 1)
+    drain(ag.values())
     for half, copies in ((0, first), (1, second)):
         landed(copies)
         merged = log_summed(rl[0, half], ra.at[0, half], 7)
@@ -330,7 +335,11 @@
             rw[1] = fac[1] / (TOTAL * summed(rl2[n, 1], rb.at[n, 1], 3))
         mass_half(1)
         ml[n] = col[...].T[0:NZ, :]
-        landed(push(ml.at[n], mr.at[n], z_peers, m_s.at[n], m_r.at[n]))
+        before = sent[:]
+        sent.clear()
+        copies = push(ml.at[n], mr.at[n], z_peers, m_s.at[n], m_r.at[n])
+        drain(before)
+        landed(copies)
         scale = 1.0 / (TOTAL * summed(ml[n], mr.at[n], 7))
         columns = jnp.concatenate([scale, jnp.zeros((CH - NZ, CH), F32)], axis=0).T
         for t in range(NZ):
@@ -380,7 +389,7 @@
     def group_end(i):
         weigh(w1, i, 7)
         multiply(w0, i, 6)
-        if i == 0:
+        if i + 1 < len(GROUPS):
             weigh(w0, i + 1, 0)
         multiply(w1, i, 7)
 
@@ -407,20 +416,33 @@
 
     part[...] = jnp.zeros((C, 128), F32)
     weigh(w0, 0, 0)
+    num[...] = jnp.zeros((NZ, CH, D), F32)
+    group(0, 0, 1)
     landed(second)
     rw[1] = fac[1] / (TOTAL * summed(rl2[2, 1], rb.at[2, 1], 3))
-    num[...] = jnp.zeros((NZ, CH, D), F32)
-    group(0, 0, 3)
+    group(0, 1, 3)
     group_end(0)
     hop(("RB", 0), 4, lo)
     hop(("LB", 0), 4, hi)
     hop(("RA", 1), 3, hi)
+    drain(sent)
+    sent.clear()
+    group(1, 0, 3)
+    group_end(1)
     hop(("LA", 1), -3, lo)
-    group(1, 0, 2)
     hop(("RB", 1), 3, lo, ("RB", 0))
     hop(("LB", 1), -3, hi, ("LB", 0))
-    group(1, 2, 3)
-    group_end(1)
+    group(2, 0, 1)
+    hop(("RA", 2), 2, hi, ("RA", 1))
+    group(2, 1, 3)
+    group_end(2)
+    hop(("LA", 2), -2, lo, ("LA", 1))
+    hop(("RB", 2), 2, lo, ("RB", 1))
+    hop(("LB", 2), -2, hi, ("LB", 1))
+    group(3, 0, 1)
+    hop(("RA", 3), 1, hi, ("RA", 2))
+    group(3, 1, 3)
+    weigh(w1, 3, 7)
     for j, q in enumerate(q for g in GROUPS for q in g):
         for i in range(16):
             rows = slice(8 * i, 8 * i + 8)
@@ -428,14 +450,13 @@
             col[rows, :] = jnp.where(lane == chunk_at(q), total, col[rows, :])
     ml[2] = col[...].T[0:NZ, :]
     last = push(ml.at[2], mr.at[2], z_peers, m_s.at[2], m_r.at[2])
-    hop(("RA", 2), 2, hi, ("RA", 1))
-    hop(("LA", 2), -2, lo, ("LA", 1))
-    hop(("RB", 2), 2, lo, ("RB", 1))
-    hop(("LB", 2), -2, hi, ("LB", 1))
-    hop(("RA", 3), 1, hi, ("RA", 2))
+    multiply(w0, 3, 6)
+    multiply(w1, 3, 7)
     hop(("LA", 3), -1, lo, ("LA", 2))
     hop(("RB", 3), 1, lo, ("RB", 2))
     hop(("LB", 3), -1, hi, ("LB", 2))
+    drain(last)
+    drain(rs.values())
 
     for copy in last:
         copy.wait_recv()
@@ -449,9 +470,6 @@
         rs[two].wait_recv()
         total = num[POS[0], rows, :] + rcv[slot[one]].astype(F32) + rcv[slot[two]].astype(F32)
         out_ref[rows, :] = (total / column[rows, :]).astype(BF16)
-
-    for copy in list(ag.values()) + sent + list(rs.values()):
-        copy.wait_send()
 
 
 def local(embeddings, centroids):

time: 101 us -> 99 us (0.980); the launches traced: 99.6 us -> 98.9 us
  no operation moved by 1% of the time
where the time goes in v6:
time: 99 us; the launch traced here: 98.9 us
  Pallas kernels  97.3 us (98%)
  local copies, waits for them, and re-layouts  1.62 us (2%)
    pallas_call x1, Pallas kernels, local(): pl.pallas_call(body, out_shape=jax.ShapeDtypeStruct((CH, D), BF16), in_sp...  97.3 us

profile of v6, /device:TPU:64, one launch (start us, length us, event | category | flops | bytes accessed | tf_op | source)
XLA Modules:
  0.0 98.9 jit_solution(4797590857350958860)
XLA Ops:
  0.0 97.3 %shard_map.28 = bf16[128,768]{1,0:T(8,128)(2,1)} custom-call(bf16[16,64,768]{2,1,0:T(8,128)(2,1)} %bitcast.5, bf16[8,4,128,768]{3,2,1,0:T(8,128)(2,1)} %bitcast.4), custom_call_target="tpu_custom_call" | custom-call | flops 12884901888 | bytes 8388608 | tf_op jit(solution)/shard_map/pallas_call | solution.py:480
  97.3 1.6 %copy.4 = bf16[1,128,768]{2,1,0:T(8,128)(2,1)} copy(bf16[1,128,768]{2,1,0:T(8,128)(2,1)} %bitcast.3) | data formatting | bytes 393216

commit v7 on v6

--- a/solution.py
+++ b/solution.py
@@ -60,97 +60,103 @@
 
     ag = {}
 
-    def plan(name, where, target, src=None):
-        i = len(ag)
+    landing = {}
+
+    def plan(name, where, target, together, src=None):
         ag[name] = pltpu.make_async_remote_copy(
-            src_ref=emb.at[where] if src is None else src, dst_ref=emb.at[where],
-            send_sem=ag_s.at[i], recv_sem=ag_r.at[i], device_id=target, device_id_type=MESH,
+            src_ref=emb.at[where] if src is None else src, dst_ref=emb.at[where], send_sem=ag_s.at[0],
+            recv_sem=ag_r.at[landing.setdefault(together, len(landing))], device_id=target, device_id_type=MESH,
         )
 
-    def plan_own(name, h, dx, s):
-        plan(name, piece(0, h, dx), at(dy=s), emb_hbm.at[h * 8 + ((x + dx + NX) % NX) * 2 + c])
-
-    plan_own(("f", 1), 1, 0, 1)
-    plan_own(("f", -1), 0, 0, -1)
-    plan_own(("g", 1), 0, 0, 1)
-    plan_own(("g", -1), 1, 0, -1)
-    plan(("y3", 1), piece(-1, 1, 0), at(dy=1))
-    plan(("y3", -1), piece(1, 0, 0), at(dy=-1))
+    def plan_own(name, h, dx, s, together):
+        plan(name, piece(0, h, dx), at(dy=s), together, emb_hbm.at[h * 8 + ((x + dx + NX) % NX) * 2 + c])
+
+    plan_own(("f", 1), 1, 0, 1, "f")
+    plan_own(("f", -1), 0, 0, -1, "f")
+    plan_own(("g", 1), 0, 0, 1, "g")
+    plan_own(("g", -1), 1, 0, -1, "g")
+    plan(("y3", 1), piece(-1, 1, 0), at(dy=1), "y3")
+    plan(("y3", -1), piece(1, 0, 0), at(dy=-1), "y3")
     for k in (1, 2, -1):
         for s in (1, -1):
-            plan_own(("k", s, k), 0, k, s)
+            plan_own(("k", s, k), 0, k, s, ("k", k > 0))
     for dy, h in ((-1, 1), (1, 1), (2, 0), (2, 1)):
         for s in (1, -1):
-            plan(("x1", s, dy, h), piece(dy, h, 0), at(dx=s))
+            key = ("x1", dy) if h == 1 and dy != 2 else ("x1", 2, (h == 0) == (s == 1))
+            plan(("x1", s, dy, h), piece(dy, h, 0), at(dx=s), key)
     for s, dy, h in ((-1, -1, 1), (1, 1, 1), (1, 2, 0), (-1, 2, 1)):
-        plan(("x2", s, dy, h), piece(dy, h, -s), at(dx=s))
+        plan(("x2", s, dy, h), piece(dy, h, -s), at(dx=s), ("x2", dy == 2))
     for dy in (-1, 1, 2):
         for h in (0, 1):
             for dx in (0, 1, 2, -1):
-                plan(("s", dy, h, dx), piece(dy, h, dx), at(flip=True))
+                plan(("s", dy, h, dx), piece(dy, h, dx), at(flip=True), ("s", dy, h))
+
+    def whole(ref, ssem, rsem):
+        return pltpu.make_async_remote_copy(
+            src_ref=ref, dst_ref=ref, send_sem=ssem, recv_sem=rsem, device_id=at(flip=True), device_id_type=MESH
+        )
 
     def send(*names):
         for name in names:
             ag[name].start()
 
-    def got(*names):
-        for name in names:
-            ag[name].wait_recv()
+    def got(together, n=2):
+        whole(emb.at[pl.ds(0, n)], ag_s.at[0], ag_r.at[landing[together]]).wait_recv()
 
     def to_sibling(*pieces):
         send(*[("s", *p) for p in pieces])
 
     def block_ready(dy, h):
-        got(*[("s", dy, h, dx) for dx in (0, 1, 2, -1)])
+        got(("s", dy, h), 4)
 
     send(("f", 1), ("f", -1), ("g", 1), ("g", -1))
     load_e.wait()
     load_c.wait()
 
     def phase_a():
-        got(("f", 1), ("f", -1))
+        got("f")
         send(("x1", 1, -1, 1), ("x1", -1, -1, 1), ("y3", 1), ("y3", -1))
         send(*[("k", s, k) for k in (1, 2, -1) for s in (1, -1)])
         to_sibling((-1, 1, 0), (1, 0, 0))
 
     def phase_c():
-        got(("g", 1), ("g", -1))
+        got("g")
         send(("x1", 1, 1, 1), ("x1", -1, 1, 1))
         to_sibling((-1, 0, 0), (1, 1, 0))
-        got(("x1", -1, -1, 1), ("x1", 1, -1, 1))
+        got(("x1", -1))
         send(("x2", -1, -1, 1))
         to_sibling((-1, 1, 1), (-1, 1, -1))
-        got(("x1", 1, 1, 1), ("x1", -1, 1, 1))
+        got(("x1", 1))
         send(("x2", 1, 1, 1))
         to_sibling((1, 1, -1), (1, 1, 1))
-        got(("y3", 1), ("y3", -1))
+        got("y3")
         send(("x1", 1, 2, 0), ("x1", -1, 2, 1), ("x1", 1, 2, 1), ("x1", -1, 2, 0))
         to_sibling((2, 1, 0), (2, 0, 0))
-        got(("x2", 1, 1, 1), ("x2", -1, -1, 1))
+        got(("x2", False))
         to_sibling((1, 1, 2), (-1, 1, 2))
         block_ready(1, 1)
 
     def phase_f():
+        got(("k", True), 4)
         for k in (1, 2):
-            got(("k", 1, k), ("k", -1, k))
             to_sibling((1, 0, k), (-1, 0, k))
         block_ready(-1, 1)
 
     def phase_g():
-        got(("x1", 1, 2, 0), ("x1", -1, 2, 1))
+        got(("x1", 2, True))
         send(("x2", 1, 2, 0), ("x2", -1, 2, 1))
         to_sibling((2, 0, -1), (2, 1, 1))
-        got(("k", 1, -1), ("k", -1, -1))
+        got(("k", False))
         to_sibling((1, 0, -1), (-1, 0, -1))
         block_ready(1, 0)
 
     def phase_h():
-        got(("x1", 1, 2, 1), ("x1", -1, 2, 0))
+        got(("x1", 2, False))
         to_sibling((2, 1, -1), (2, 0, 1))
         block_ready(-1, 0)
 
     def phase_i():
-        got(("x2", 1, 2, 0), ("x2", -1, 2, 1))
+        got(("x2", True))
         to_sibling((2, 0, 2), (2, 1, 2))
         block_ready(2, 0)
 
@@ -160,28 +166,27 @@
     sent = []
 
     def push(src, dst, peers, ssem, rsem, start=True):
-        copies = []
-        for k, peer in enumerate(peers):
-            copy = pltpu.make_async_remote_copy(
-                src_ref=src, dst_ref=dst.at[k], send_sem=ssem.at[k], recv_sem=rsem.at[k],
-                device_id=peer, device_id_type=MESH,
+        copies = [
+            pltpu.make_async_remote_copy(
+                src_ref=src, dst_ref=dst.at[k], send_sem=ssem, recv_sem=rsem, device_id=peer, device_id_type=MESH
             )
-            copies.append(copy)
-        sent.extend(copies)
+            for k, peer in enumerate(peers)
+        ]
         if start:
             begin(copies)
-        return copies
+        both = whole(dst, ssem, rsem)
+        sent.append(both)
+        return both, copies
 
     def begin(copies):
         for copy in copies:
             copy.start()
 
-    def landed(copies):
-        for copy in copies:
-            copy.wait_recv()
-
-    def drain(copies):
-        for copy in copies:
+    def landed(pushed):
+        pushed[0].wait_recv()
+
+    def drain(wholes):
+        for copy in wholes:
             copy.wait_send()
 
     def push_1(n, half, start=True):
@@ -253,7 +258,7 @@
 
         @pl.when(p == 2)
         def _():
-            begin(first)
+            begin(first[1])
             phase_h()
 
         pl.when(p == 3)(phase_j)
@@ -263,7 +268,7 @@
     high = lax.fori_loop(0, 4, two_steps, jnp.zeros((8, BW), F32))
     step(None, None, buf1, place_of(3, True), high, 1, 6)
     second = push_1(0, 1)
-    drain(ag.values())
+    whole(emb.at[pl.ds(0, 48)], ag_s.at[0], ag_r.at[0]).wait_send()
     for half, copies in ((0, first), (1, second)):
         landed(copies)
         merged = log_summed(rl[0, half], ra.at[0, half], 7)
@@ -405,7 +410,7 @@
         snd[i] = value.astype(BF16)
         slot[name] = i
         copy = pltpu.make_async_remote_copy(
-            src_ref=snd.at[i], dst_ref=rcv.at[i], send_sem=rs_s.at[i], recv_sem=rs_r.at[i],
+            src_ref=snd.at[i], dst_ref=rcv.at[i], send_sem=rs_s.at[0], recv_sem=rs_r.at[i],
             device_id=at(dz=sign), device_id_type=MESH,
         )
         copy.start()
@@ -455,11 +460,10 @@
     hop(("LA", 3), -1, lo, ("LA", 2))
     hop(("RB", 3), 1, lo, ("RB", 2))
     hop(("LB", 3), -1, hi, ("LB", 2))
-    drain(last)
-    drain(rs.values())
-
-    for copy in last:
-        copy.wait_recv()
+    drain(last[:1])
+    whole(snd, rs_s.at[0], rs_r.at[0]).wait_send()
+
+    landed(last)
     mass = ml[2, pl.ds(z, 1), :]
     for k in range(7):
         mass = mass + mr[2, k, pl.ds(z, 1), :]
@@ -490,8 +494,8 @@
             v((3, NZ, CH), F32), v((3, 7, NZ, CH), F32),
             v((GROUP * CH, BW), BF16), v((GROUP * CH, BW), BF16), v((NZ, CH, D), F32),
             v((14, 64, D), BF16), v((14, 64, D), BF16),
-            dma((2,)), dma((48,)), dma((48,)), dma((3, 2, 7)), dma((3, 2, 7)), dma((3, 2, 3)), dma((3, 2, 3)),
-            dma((3, 7)), dma((3, 7)), dma((14,)), dma((14,)),
+            dma((2,)), dma((1,)), dma((17,)), dma((3, 2)), dma((3, 2)), dma((3, 2)), dma((3, 2)),
+            dma((3,)), dma((3,)), dma((1,)), dma((14,)),
         ],
         compiler_params=pltpu.CompilerParams(
             collective_id=0, has_side_effects=True, vmem_limit_bytes=60 * 1024 * 1024

time: 99 us -> 97 us (0.980)
  Pallas kernels: 97.3 us -> 95.3 us
    pallas_call x1, Pallas kernels: 97.3 us -> 95.3 us  [local(): pl.pallas_call(body, out_shape=jax.ShapeDtypeStruct((CH, D), BF16), in_sp...]
where the time goes in v7:
time: 97 us; the launch traced here: 96.9 us
  Pallas kernels  95.3 us (98%)
  local copies, waits for them, and re-layouts  1.62 us (2%)
    pallas_call x1, Pallas kernels, local(): pl.pallas_call(body, out_shape=jax.ShapeDtypeStruct((CH, D), BF16), in_sp...  95.3 us

profile of v7, /device:TPU:64, one launch (start us, length us, event | category | flops | bytes accessed | tf_op | source)
XLA Modules:
  0.0 96.9 jit_solution(14099702063843836111)
XLA Ops:
  0.0 95.3 %shard_map.28 = bf16[128,768]{1,0:T(8,128)(2,1)} custom-call(bf16[16,64,768]{2,1,0:T(8,128)(2,1)} %bitcast.5, bf16[8,4,128,768]{3,2,1,0:T(8,128)(2,1)} %bitcast.4), custom_call_target="tpu_custom_call" | custom-call | flops 12884901888 | bytes 8388608 | tf_op jit(solution)/shard_map/pallas_call | solution.py:484
  95.3 1.6 %copy.4 = bf16[1,128,768]{2,1,0:T(8,128)(2,1)} copy(bf16[1,128,768]{2,1,0:T(8,128)(2,1)} %bitcast.3) | data formatting | bytes 393216

commit v8 on v7

--- a/solution.py
+++ b/solution.py
@@ -79,13 +79,13 @@
     plan(("y3", -1), piece(1, 0, 0), at(dy=-1), "y3")
     for k in (1, 2, -1):
         for s in (1, -1):
-            plan_own(("k", s, k), 0, k, s, ("k", k > 0))
+            plan_own(("k", s, k), 0, k, s, ("k", k))
     for dy, h in ((-1, 1), (1, 1), (2, 0), (2, 1)):
         for s in (1, -1):
             key = ("x1", dy) if h == 1 and dy != 2 else ("x1", 2, (h == 0) == (s == 1))
             plan(("x1", s, dy, h), piece(dy, h, 0), at(dx=s), key)
     for s, dy, h in ((-1, -1, 1), (1, 1, 1), (1, 2, 0), (-1, 2, 1)):
-        plan(("x2", s, dy, h), piece(dy, h, -s), at(dx=s), ("x2", dy == 2))
+        plan(("x2", s, dy, h), piece(dy, h, -s), at(dx=s), ("x2", dy))
     for dy in (-1, 1, 2):
         for h in (0, 1):
             for dx in (0, 1, 2, -1):
@@ -109,54 +109,56 @@
     def block_ready(dy, h):
         got(("s", dy, h), 4)
 
-    send(("f", 1), ("f", -1), ("g", 1), ("g", -1))
+    send(("f", 1), ("f", -1))
     load_e.wait()
     load_c.wait()
 
     def phase_a():
+        send(("g", 1), ("g", -1))
         got("f")
-        send(("x1", 1, -1, 1), ("x1", -1, -1, 1), ("y3", 1), ("y3", -1))
-        send(*[("k", s, k) for k in (1, 2, -1) for s in (1, -1)])
+        send(("y3", 1), ("y3", -1), ("x1", 1, -1, 1), ("x1", -1, -1, 1))
         to_sibling((-1, 1, 0), (1, 0, 0))
 
     def phase_c():
         got("g")
-        send(("x1", 1, 1, 1), ("x1", -1, 1, 1))
+        send(("x1", 1, 1, 1), ("x1", -1, 1, 1), ("k", 1, 1), ("k", -1, 1))
         to_sibling((-1, 0, 0), (1, 1, 0))
         got(("x1", -1))
         send(("x2", -1, -1, 1))
         to_sibling((-1, 1, 1), (-1, 1, -1))
+        got("y3")
+        send(("x1", 1, 2, 0), ("x1", -1, 2, 1), ("k", 1, 2), ("k", -1, 2))
+        to_sibling((2, 1, 0), (2, 0, 0))
         got(("x1", 1))
-        send(("x2", 1, 1, 1))
+        send(("x2", 1, 1, 1), ("x1", 1, 2, 1), ("x1", -1, 2, 0), ("k", 1, -1), ("k", -1, -1))
         to_sibling((1, 1, -1), (1, 1, 1))
-        got("y3")
-        send(("x1", 1, 2, 0), ("x1", -1, 2, 1), ("x1", 1, 2, 1), ("x1", -1, 2, 0))
-        to_sibling((2, 1, 0), (2, 0, 0))
-        got(("x2", False))
-        to_sibling((1, 1, 2), (-1, 1, 2))
-        block_ready(1, 1)
+        got(("x2", -1), 1)
+        to_sibling((-1, 1, 2))
+        block_ready(-1, 1)
 
     def phase_f():
-        got(("k", True), 4)
         for k in (1, 2):
+            got(("k", k))
             to_sibling((1, 0, k), (-1, 0, k))
-        block_ready(-1, 1)
-
-    def phase_g():
         got(("x1", 2, True))
         send(("x2", 1, 2, 0), ("x2", -1, 2, 1))
         to_sibling((2, 0, -1), (2, 1, 1))
-        got(("k", False))
+        got(("x2", 1), 1)
+        to_sibling((1, 1, 2))
+        block_ready(1, 1)
+
+    def phase_g():
+        got(("k", -1))
         to_sibling((1, 0, -1), (-1, 0, -1))
-        block_ready(1, 0)
+        block_ready(-1, 0)
 
     def phase_h():
         got(("x1", 2, False))
         to_sibling((2, 1, -1), (2, 0, 1))
-        block_ready(-1, 0)
+        block_ready(1, 0)
 
     def phase_i():
-        got(("x2", True))
+        got(("x2", 2))
         to_sibling((2, 0, 2), (2, 1, 2))
         block_ready(2, 0)
 
@@ -213,8 +215,8 @@
     def place_of(p, odd):
         d = (p + 1) // 2
         if odd:
-            return ((y - d + NY) % NY) * 2 + 1 - (1 - p % 2) * (p // 2)
-        return ((y + d) % NY) * 2 + (p % 2) * (1 - p // 2)
+            return ((y + d) % NY) * 2 + 1 - (1 - p % 2) * (p // 2)
+        return ((y - d + NY) % NY) * 2 + (p % 2) * (1 - p // 2)
 
     def step(new_buf, new, old_buf, old, old_max, half, row):
         top = jnp.max(old_max, axis=0, keepdims=True)
@@ -429,22 +431,23 @@
     group_end(0)
     hop(("RB", 0), 4, lo)
     hop(("LB", 0), 4, hi)
-    hop(("RA", 1), 3, hi)
     drain(sent)
     sent.clear()
-    group(1, 0, 3)
+    group(1, 0, 1)
+    hop(("RA", 1), 3, hi)
+    group(1, 1, 3)
     group_end(1)
+    hop(("RB", 1), 3, lo, ("RB", 0))
     hop(("LA", 1), -3, lo)
-    hop(("RB", 1), 3, lo, ("RB", 0))
+    group(2, 0, 1)
     hop(("LB", 1), -3, hi, ("LB", 0))
-    group(2, 0, 1)
     hop(("RA", 2), 2, hi, ("RA", 1))
     group(2, 1, 3)
     group_end(2)
+    hop(("RB", 2), 2, lo, ("RB", 1))
     hop(("LA", 2), -2, lo, ("LA", 1))
-    hop(("RB", 2), 2, lo, ("RB", 1))
+    group(3, 0, 1)
     hop(("LB", 2), -2, hi, ("LB", 1))
-    group(3, 0, 1)
     hop(("RA", 3), 1, hi, ("RA", 2))
     group(3, 1, 3)
     weigh(w1, 3, 7)
@@ -457,8 +460,8 @@
     last = push(ml.at[2], mr.at[2], z_peers, m_s.at[2], m_r.at[2])
     multiply(w0, 3, 6)
     multiply(w1, 3, 7)
+    hop(("RB", 3), 1, lo, ("RB", 2))
     hop(("LA", 3), -1, lo, ("LA", 2))
-    hop(("RB", 3), 1, lo, ("RB", 2))
     hop(("LB", 3), -1, hi, ("LB", 2))
     drain(last[:1])
     whole(snd, rs_s.at[0], rs_r.at[0]).wait_send()
@@ -494,7 +497,7 @@
             v((3, NZ, CH), F32), v((3, 7, NZ, CH), F32),
             v((GROUP * CH, BW), BF16), v((GROUP * CH, BW), BF16), v((NZ, CH, D), F32),
             v((14, 64, D), BF16), v((14, 64, D), BF16),
-            dma((2,)), dma((1,)), dma((17,)), dma((3, 2)), dma((3, 2)), dma((3, 2)), dma((3, 2)),
+            dma((2,)), dma((1,)), dma((20,)), dma((3, 2)), dma((3, 2)), dma((3, 2)), dma((3, 2)),
             dma((3,)), dma((3,)), dma((1,)), dma((14,)),
         ],
         compiler_params=pltpu.CompilerParams(

time: 97 us -> 97.3 us (level)
  no operation moved by 1% of the time
where the time goes in v8:
time: 97.3 us; the launch traced here: 97.2 us
  Pallas kernels  95.6 us (98%)
  local copies, waits for them, and re-layouts  1.62 us (2%)
    pallas_call x1, Pallas kernels, local(): pl.pallas_call(body, out_shape=jax.ShapeDtypeStruct((CH, D), BF16), in_sp...  95.6 us

profile of v8, /device:TPU:64, one launch (start us, length us, event | category | flops | bytes accessed | tf_op | source)
XLA Modules:
  0.0 97.2 jit_solution(15215110628228984659)
XLA Ops:
  0.0 95.6 %shard_map.28 = bf16[128,768]{1,0:T(8,128)(2,1)} custom-call(bf16[16,64,768]{2,1,0:T(8,128)(2,1)} %bitcast.5, bf16[8,4,128,768]{3,2,1,0:T(8,128)(2,1)} %bitcast.4), custom_call_target="tpu_custom_call" | custom-call | flops 12884901888 | bytes 8388608 | tf_op jit(solution)/shard_map/pallas_call | solution.py:487
  95.6 1.6 %copy.4 = bf16[1,128,768]{2,1,0:T(8,128)(2,1)} copy(bf16[1,128,768]{2,1,0:T(8,128)(2,1)} %bitcast.3) | data formatting | bytes 393216

commit v9 on v8

--- a/solution.py
+++ b/solution.py
@@ -267,8 +267,9 @@
         return step(buf1, place_of(p, True), buf0, place_of(p, False), high, p // 2, (p % 2) * 4)
 
     buf1[...] = jnp.zeros((C, BW), F32)
-    high = lax.fori_loop(0, 4, two_steps, jnp.zeros((8, BW), F32))
-    step(None, None, buf1, place_of(3, True), high, 1, 6)
+    with jax.named_scope("logits"):
+        high = lax.fori_loop(0, 4, two_steps, jnp.zeros((8, BW), F32))
+        step(None, None, buf1, place_of(3, True), high, 1, 6)
     second = push_1(0, 1)
     whole(emb.at[pl.ds(0, 48)], ag_s.at[0], ag_r.at[0]).wait_send()
     for half, copies in ((0, first), (1, second)):
@@ -334,13 +335,15 @@
 
     col[...] = jnp.zeros((CH, CH), F32)
     for n in range(2):
-        mass_half(0)
+        with jax.named_scope("mass"):
+            mass_half(0)
         landed(second)
         if n == 0:
             start_weights(1)
         else:
             rw[1] = fac[1] / (TOTAL * summed(rl2[n, 1], rb.at[n, 1], 3))
-        mass_half(1)
+        with jax.named_scope("mass"):
+            mass_half(1)
         ml[n] = col[...].T[0:NZ, :]
         before = sent[:]
         sent.clear()
@@ -351,9 +354,11 @@
         columns = jnp.concatenate([scale, jnp.zeros((CH - NZ, CH), F32)], axis=0).T
         for t in range(NZ):
             scol[t * CH:(t + 1) * CH, :] = jnp.broadcast_to(columns[:, t:t + 1], (CH, CH))
-        row_half(n + 1, 0)
+        with jax.named_scope("rows"):
+            row_half(n + 1, 0)
         first = push_1(n + 1, 0)
-        row_half(n + 1, 1)
+        with jax.named_scope("rows"):
+            row_half(n + 1, 1)
         second = push_1(n + 1, 1)
         landed(first)
         rl2[n + 1, 0] = summed(rl[n + 1, 0], ra.at[n + 1, 0], 7)
@@ -391,7 +396,8 @@
             multiply(w1, i, 2 * k + 1)
             return 0
 
-        lax.fori_loop(start, stop, two, 0)
+        with jax.named_scope("numerators"):
+            lax.fori_loop(start, stop, two, 0)
 
     def group_end(i):
         weigh(w1, i, 7)
@@ -403,20 +409,21 @@
     rs = {}
 
     def hop(name, q, rows, before=None):
-        sign = (1 if name[0] in ("RA", "RB") else -1)
-        i = len(rs)
-        value = num[POS[q], rows, :]
-        if before is not None:
-            rs[before].wait_recv()
-            value = value + rcv[slot[before]].astype(F32)
-        snd[i] = value.astype(BF16)
-        slot[name] = i
-        copy = pltpu.make_async_remote_copy(
-            src_ref=snd.at[i], dst_ref=rcv.at[i], send_sem=rs_s.at[0], recv_sem=rs_r.at[i],
-            device_id=at(dz=sign), device_id_type=MESH,
-        )
-        copy.start()
-        rs[name] = copy
+        sign = 1 if name[0] in ("RA", "RB") else -1
+        for part_of in range(2):
+            i = len(rs)
+            value = num[POS[q], rows.start + 32 * part_of:rows.start + 32 * part_of + 32, :]
+            if before is not None:
+                rs[(*before, part_of)].wait_recv()
+                value = value + rcv[slot[(*before, part_of)]].astype(F32)
+            snd[i] = value.astype(BF16)
+            slot[(*name, part_of)] = i
+            copy = pltpu.make_async_remote_copy(
+                src_ref=snd.at[i], dst_ref=rcv.at[i], send_sem=rs_s.at[0], recv_sem=rs_r.at[i],
+                device_id=at(dz=sign), device_id_type=MESH,
+            )
+            copy.start()
+            rs[(*name, part_of)] = copy
 
     slot = {}
     lo, hi = slice(0, 64), slice(64, 128)
@@ -466,17 +473,23 @@
     drain(last[:1])
     whole(snd, rs_s.at[0], rs_r.at[0]).wait_send()
 
-    landed(last)
+    with jax.named_scope("last_hops"):
+        landed(last)
+        rs[("RB", 3, 0)].wait_recv()
     mass = ml[2, pl.ds(z, 1), :]
     for k in range(7):
         mass = mass + mr[2, k, pl.ds(z, 1), :]
     column = jnp.broadcast_to(mass, (CH, CH)).T
     column = jnp.concatenate([column] * (D // CH), axis=1)
-    for rows, one, two in ((hi, ("RA", 3), ("LB", 3)), (lo, ("LA", 3), ("RB", 3))):
-        rs[one].wait_recv()
-        rs[two].wait_recv()
-        total = num[POS[0], rows, :] + rcv[slot[one]].astype(F32) + rcv[slot[two]].astype(F32)
-        out_ref[rows, :] = (total / column[rows, :]).astype(BF16)
+    for start, one, two in ((64, ("RA", 3), ("LB", 3)), (0, ("LA", 3), ("RB", 3))):
+        for part_of in range(2):
+            rows = slice(start + 32 * part_of, start + 32 * part_of + 32)
+            total = num[POS[0], rows, :]
+            for name in (one, two):
+                if (*name, part_of) != ("RB", 3, 0):
+                    rs[(*name, part_of)].wait_recv()
+                total = total + rcv[slot[(*name, part_of)]].astype(F32)
+            out_ref[rows, :] = (total / column[rows, :]).astype(BF16)
 
 
 def local(embeddings, centroids):
@@ -496,9 +509,9 @@
             v((2, 8, 256), F32), v((2, 8, 256), F32), v((C, 128), F32), v((C, 128), F32), v((CH, CH), F32),
             v((3, NZ, CH), F32), v((3, 7, NZ, CH), F32),
             v((GROUP * CH, BW), BF16), v((GROUP * CH, BW), BF16), v((NZ, CH, D), F32),
-            v((14, 64, D), BF16), v((14, 64, D), BF16),
+            v((28, 32, D), BF16), v((28, 32, D), BF16),
             dma((2,)), dma((1,)), dma((20,)), dma((3, 2)), dma((3, 2)), dma((3, 2)), dma((3, 2)),
-            dma((3,)), dma((3,)), dma((1,)), dma((14,)),
+            dma((3,)), dma((3,)), dma((1,)), dma((28,)),
         ],
         compiler_params=pltpu.CompilerParams(
             collective_id=0, has_side_effects=True, vmem_limit_bytes=60 * 1024 * 1024

time: 97.3 us -> 97 us (level)
  no operation moved by 1% of the time
where the time goes in v9:
time: 97 us; the launch traced here: 96.9 us
  Pallas kernels  95.3 us (98%)
  local copies, waits for them, and re-layouts  1.62 us (2%)
    pallas_call x1, Pallas kernels, local(): pl.pallas_call(body, out_shape=jax.ShapeDtypeStruct((CH, D), BF16), in_sp...  95.3 us

profile of v9, /device:TPU:64, one launch (start us, length us, event | category | flops | bytes accessed | tf_op | source)
XLA Modules:
  0.0 96.9 jit_solution(11126183716635781915)
XLA Ops:
  0.0 95.3 %shard_map.28 = bf16[128,768]{1,0:T(8,128)(2,1)} custom-call(bf16[16,64,768]{2,1,0:T(8,128)(2,1)} %bitcast.5, bf16[8,4,128,768]{3,2,1,0:T(8,128)(2,1)} %bitcast.4), custom_call_target="tpu_custom_call" | custom-call | flops 12884901888 | bytes 8388608 | tf_op jit(solution)/shard_map/pallas_call | solution.py:500
  95.3 1.6 %copy.4 = bf16[1,128,768]{2,1,0:T(8,128)(2,1)} copy(bf16[1,128,768]{2,1,0:T(8,128)(2,1)} %bitcast.3) | data formatting | bytes 393216

commit v10 on v9

--- a/solution.py
+++ b/solution.py
@@ -19,8 +19,8 @@
 TOTAL = 32768.0
 EXP2_SCALE = 10.0 * float(np.log2(np.e))
 
-GROUPS = ((4, 3), (-3, 2), (-2, 1), (-1, 0))
-GROUP = len(GROUPS[0])
+GROUPS = ((4,), (3, -3), (2, -2), (1, -1), (0,))
+GROUP = 2
 POS = {q: i for i, q in enumerate(q for group in GROUPS for q in group)}
 LN2 = float(np.log(2.0))
 
@@ -376,7 +376,7 @@
         ws = [rw[b // 4, pl.ds((b % 4) * 2 + j, 1), :] for j in range(2)]
         for j, q in enumerate(GROUPS[i]):
             rows = pl.ds(pl.multiple_of(chunk_at(q) * CH, CH), CH)
-            place = slice((GROUP * i + j) * CH, (GROUP * i + j + 1) * CH)
+            place = slice(POS[q] * CH, (POS[q] + 1) * CH)
             acc = part[place, :]
             for l in range(BW // 128):
                 value = kern[b, rows, l * 128:l * 128 + 128] * ws[l // 2][:, (l % 2) * 128:(l % 2) * 128 + 128]
@@ -386,7 +386,8 @@
 
     def multiply(w, i, b):
         e = emb[pl.ds(b * 8, 8)].reshape(BW, D)
-        num[GROUP * i:GROUP * i + GROUP] += jnp.dot(w[...], e, preferred_element_type=F32).reshape(GROUP, CH, D)
+        n, first = len(GROUPS[i]), POS[GROUPS[i][0]]
+        num[first:first + n] += jnp.dot(w[0:n * CH, :], e, preferred_element_type=F32).reshape(n, CH, D)
 
     def group(i, start, stop):
         def two(k, _):
@@ -440,24 +441,26 @@
     hop(("LB", 0), 4, hi)
     drain(sent)
     sent.clear()
-    group(1, 0, 1)
+    group(1, 0, 3)
+    group_end(1)
     hop(("RA", 1), 3, hi)
-    group(1, 1, 3)
-    group_end(1)
-    hop(("RB", 1), 3, lo, ("RB", 0))
     hop(("LA", 1), -3, lo)
     group(2, 0, 1)
+    hop(("RB", 1), 3, lo, ("RB", 0))
     hop(("LB", 1), -3, hi, ("LB", 0))
-    hop(("RA", 2), 2, hi, ("RA", 1))
     group(2, 1, 3)
     group_end(2)
+    hop(("RA", 2), 2, hi, ("RA", 1))
+    hop(("LA", 2), -2, lo, ("LA", 1))
+    group(3, 0, 2)
     hop(("RB", 2), 2, lo, ("RB", 1))
-    hop(("LA", 2), -2, lo, ("LA", 1))
-    group(3, 0, 1)
     hop(("LB", 2), -2, hi, ("LB", 1))
+    group(3, 2, 3)
+    group_end(3)
     hop(("RA", 3), 1, hi, ("RA", 2))
-    group(3, 1, 3)
-    weigh(w1, 3, 7)
+    hop(("LA", 3), -1, lo, ("LA", 2))
+    group(4, 0, 3)
+    weigh(w1, 4, 7)
     for j, q in enumerate(q for g in GROUPS for q in g):
         for i in range(16):
             rows = slice(8 * i, 8 * i + 8)
@@ -465,10 +468,9 @@
             col[rows, :] = jnp.where(lane == chunk_at(q), total, col[rows, :])
     ml[2] = col[...].T[0:NZ, :]
     last = push(ml.at[2], mr.at[2], z_peers, m_s.at[2], m_r.at[2])
-    multiply(w0, 3, 6)
-    multiply(w1, 3, 7)
+    multiply(w0, 4, 6)
+    multiply(w1, 4, 7)
     hop(("RB", 3), 1, lo, ("RB", 2))
-    hop(("LA", 3), -1, lo, ("LA", 2))
     hop(("LB", 3), -1, hi, ("LB", 2))
     drain(last[:1])
     whole(snd, rs_s.at[0], rs_r.at[0]).wait_send()

time: 97 us -> 95.1 us (0.980); the launches traced: 96.9 us -> 93.8 us
  Pallas kernels: 95.3 us -> 92.1 us
    pallas_call x1, Pallas kernels: 95.3 us -> 92.1 us  [local(): pl.pallas_call(body, out_shape=jax.ShapeDtypeStruct((CH, D), BF16), in_sp...]
where the time goes in v10:
time: 95.1 us; the launch traced here: 93.8 us
  Pallas kernels  92.1 us (97%)
  local copies, waits for them, and re-layouts  1.62 us (2%)
    pallas_call x1, Pallas kernels, local(): pl.pallas_call(body, out_shape=jax.ShapeDtypeStruct((CH, D), BF16), in_sp...  92.1 us

profile of v10, /device:TPU:64, one launch (start us, length us, event | category | flops | bytes accessed | tf_op | source)
XLA Modules:
  0.0 93.8 jit_solution(3683368661831515207)
XLA Ops:
  0.0 92.1 %shard_map.28 = bf16[128,768]{1,0:T(8,128)(2,1)} custom-call(bf16[16,64,768]{2,1,0:T(8,128)(2,1)} %bitcast.5, bf16[8,4,128,768]{3,2,1,0:T(8,128)(2,1)} %bitcast.4), custom_call_target="tpu_custom_call" | custom-call | flops 12884901888 | bytes 8388608 | tf_op jit(solution)/shard_map/pallas_call | solution.py:502
  92.1 1.6 %copy.4 = bf16[1,128,768]{2,1,0:T(8,128)(2,1)} copy(bf16[1,128,768]{2,1,0:T(8,128)(2,1)} %bitcast.3) | data formatting | bytes 393216

commit v11 on v10

--- a/solution.py
+++ b/solution.py
@@ -110,6 +110,7 @@
         got(("s", dy, h), 4)
 
     send(("f", 1), ("f", -1))
+    buf1[...] = jnp.zeros((C, BW), F32)
     load_e.wait()
     load_c.wait()
 
@@ -266,7 +267,6 @@
         pl.when(p == 3)(phase_j)
         return step(buf1, place_of(p, True), buf0, place_of(p, False), high, p // 2, (p % 2) * 4)
 
-    buf1[...] = jnp.zeros((C, BW), F32)
     with jax.named_scope("logits"):
         high = lax.fori_loop(0, 4, two_steps, jnp.zeros((8, BW), F32))
         step(None, None, buf1, place_of(3, True), high, 1, 6)
@@ -349,6 +349,10 @@
         sent.clear()
         copies = push(ml.at[n], mr.at[n], z_peers, m_s.at[n], m_r.at[n])
         drain(before)
+        if n == 0:
+            num[...] = jnp.zeros((NZ, CH, D), F32)
+        else:
+            part[...] = jnp.zeros((C, 128), F32)
         landed(copies)
         scale = 1.0 / (TOTAL * summed(ml[n], mr.at[n], 7))
         columns = jnp.concatenate([scale, jnp.zeros((CH - NZ, CH), F32)], axis=0).T
@@ -429,9 +433,7 @@
     slot = {}
     lo, hi = slice(0, 64), slice(64, 128)
 
-    part[...] = jnp.zeros((C, 128), F32)
     weigh(w0, 0, 0)
-    num[...] = jnp.zeros((NZ, CH, D), F32)
     group(0, 0, 1)
     landed(second)
     rw[1] = fac[1] / (TOTAL * summed(rl2[2, 1], rb.at[2, 1], 3))

time: 95.1 us -> 95.4 us (level)
  no operation moved by 1% of the time
where the time goes in v11:
time: 95.4 us; the launch traced here: 93.8 us
  Pallas kernels  92.2 us (97%)
  local copies, waits for them, and re-layouts  1.62 us (2%)
    pallas_call x1, Pallas kernels, local(): pl.pallas_call(body, out_shape=jax.ShapeDtypeStruct((CH, D), BF16), in_sp...  92.2 us

profile of v11, /device:TPU:64, one launch (start us, length us, event | category | flops | bytes accessed | tf_op | source)
XLA Modules:
  0.0 93.8 jit_solution(17405438113729507413)
XLA Ops:
  0.0 92.2 %shard_map.28 = bf16[128,768]{1,0:T(8,128)(2,1)} custom-call(bf16[16,64,768]{2,1,0:T(8,128)(2,1)} %bitcast.5, bf16[8,4,128,768]{3,2,1,0:T(8,128)(2,1)} %bitcast.4), custom_call_target="tpu_custom_call" | custom-call | flops 12884901888 | bytes 8388608 | tf_op jit(solution)/shard_map/pallas_call | solution.py:504
  92.2 1.6 %copy.4 = bf16[1,128,768]{2,1,0:T(8,128)(2,1)} copy(bf16[1,128,768]{2,1,0:T(8,128)(2,1)} %bitcast.3) | data formatting | bytes 393216
